TPU v7x, 512 devices: a whole 4x8x8 slice. The times are simulated.
512 devices in a mesh: rows: 128 (over x_hi, y, z), cols: 4 (over x_lo, core).
Axes of the slice: x: 4 (x_hi: 2, x_lo: 2; x = x_hi * 2 + x_lo), y: 8, z: 8, core: 2. Of those that a mesh axis runs over, the one named last changes fastest.
Arguments:
- trace_limbs: float32 [2, 33554432], P(None, ('cols', 'rows')), parts along dimension 1, may hold values from 0 to 1, as said below
- coset_shift: int32 [1], replicated, may hold values from 1 to 2013265920
Outputs:
- extension: float32 [2, 67108864], P(None, ('cols', 'rows')), parts along dimension 1
There are 4 independent parts, one for each index of `cols`. A program takes and returns all parts, laid end to end along the dimension named above; an argument that names none is the same for every part. Nothing has to cross between parts.
Inputs may be any that keep to these rules, and one draw needn't show every extreme that they name: `trace_limbs`: every entry is a whole multiple of 2**-16, and the entries of the second limb row are below one half.
All inputs are finite; a program needn't handle non-finite values.
Results may differ from a plain program's by a relative error of at most 0.0003.
Values may be sent and summed in bfloat16 or wider, within the bound.
No kernel may reach another device: no remote copies, remote signals or barrier semaphores. Data moves between devices by JAX's collectives and lax.ppermute only.
A program may use at most 128 MiB of HBM per device.

v0:
```python
import jax
import jax.numpy as jnp
from jax import lax
from jax.sharding import PartitionSpec as P

LEN_A = 2048
LEN_B = 4096


MODULUS = 2013265921


def unity_root(length):
    return pow(pow(31, 15, MODULUS), (1 << 27) // length, MODULUS)


def reduce_product(small_factor, field_factor):
    estimate = jnp.floor(
        small_factor.astype(jnp.float32) * field_factor.astype(jnp.float32) * (1.0 / MODULUS) + 0.5
    )
    remainder = small_factor * field_factor - estimate.astype(jnp.int32) * MODULUS
    return jnp.where(remainder < 0, remainder + MODULUS, remainder)


def field_add(first_term, second_term):
    summed = first_term - MODULUS + second_term
    return jnp.where(summed < 0, summed + MODULUS, summed)


def field_sub(first_term, second_term):
    differ = first_term - second_term
    return jnp.where(differ < 0, differ + MODULUS, differ)


def field_mul(factor_one, factor_two):
    high_part = reduce_product(factor_one >> 16, factor_two)
    low_part = reduce_product(factor_one & 65535, factor_two)
    return field_add(reduce_product(jnp.int32(65536), high_part), low_part)


def paired_mul(factor_one, table_plain, table_lifted):
    high_part = reduce_product(factor_one >> 16, table_lifted)
    low_part = reduce_product(factor_one & 65535, table_plain)
    return field_add(high_part, low_part)


def const_powers(base_value, exponents, bit_count):
    result = jnp.ones_like(exponents)
    for bit_level in range(bit_count):
        factor = jnp.where(
            exponents >> bit_level & 1 == 1,
            jnp.int32(pow(base_value, 1 << bit_level, MODULUS)),
            jnp.int32(1),
        )
        result = field_mul(result, factor)
    return result


def traced_powers(base_value, exponents, bit_count):
    result = jnp.ones_like(exponents)
    square = base_value
    for bit_level in range(bit_count):
        result = jnp.where(exponents >> bit_level & 1 == 1, field_mul(result, square), result)
        square = field_mul(square, square)
    return result


def power_table(base_value, length):
    low_count = min(64, length)
    low_part = const_powers(base_value, jnp.arange(low_count, dtype=jnp.int32), 6)
    high_count = length // low_count
    high_part = const_powers(
        pow(base_value, low_count, MODULUS),
        jnp.arange(high_count, dtype=jnp.int32),
        max(1, high_count.bit_length()),
    )
    plain = field_mul(high_part[:, None], low_part[None, :]).reshape(length)
    return (plain, field_mul(plain, jnp.int32(65536)))


def transform(values, root_pair):
    table_plain, table_lifted = root_pair
    length = values.shape[-1]
    row_count = values.size // length
    state = values.reshape(row_count, length)
    leading = state.T.reshape(1, length * row_count)
    half_span = 1
    while half_span < length and half_span < 128:
        groups = length // (2 * half_span)
        halves = leading.reshape(half_span, 2, groups * row_count)
        even_part = halves[:, 0]
        odd_part = halves[:, 1]
        product = paired_mul(
            odd_part, table_plain[::groups][:, None], table_lifted[::groups][:, None]
        )
        leading = jnp.stack(
            [field_add(even_part, product), field_sub(even_part, product)], 0
        ).reshape(2 * half_span, groups * row_count)
        half_span = half_span * 2
    state = (
        leading.reshape(half_span, length // half_span, row_count)
        .transpose(2, 1, 0)
        .reshape(row_count, length)
    )
    while half_span < length:
        groups = length // (2 * half_span)
        halves = state.reshape(row_count, 2, length // 2)
        even_part = halves[:, 0]
        odd_part = halves[:, 1]
        plain_row = jnp.tile(table_plain[::groups], groups)
        lifted_row = jnp.tile(table_lifted[::groups], groups)
        product = paired_mul(odd_part, plain_row[None, :], lifted_row[None, :])
        sum_part = field_add(even_part, product).reshape(row_count, groups, half_span)
        diff_part = field_sub(even_part, product).reshape(row_count, groups, half_span)
        state = jnp.stack([sum_part, diff_part], 2).reshape(row_count, length)
        half_span = half_span * 2
    return state.reshape(values.shape)


def cross_twiddle(root_value, line_ids, width, modulus_len):
    bit_count = (modulus_len - 1).bit_length()
    fine_exp = jnp.arange(64, dtype=jnp.int32)
    coarse = jnp.arange(width // 64, dtype=jnp.int32) * 64
    fine_part = const_powers(
        root_value, line_ids[:, None] * fine_exp[None, :] & modulus_len - 1, bit_count
    )
    coarse_part = const_powers(
        root_value, line_ids[:, None] * coarse[None, :] & modulus_len - 1, bit_count
    )
    return field_mul(coarse_part[:, :, None], fine_part[:, None, :]).reshape(
        line_ids.shape[0], width
    )


def from_limbs(trace_limbs):
    low_part = (trace_limbs[0] * 65536.0).astype(jnp.int32)
    high_part = (trace_limbs[1] * 65536.0).astype(jnp.int32)
    joined = high_part * 65536 + low_part
    return jnp.where(joined >= MODULUS, joined - MODULUS, joined)


def to_limbs(field_values):
    return (
        jnp.stack(
            [(field_values & 65535).astype(jnp.float32), (field_values >> 16).astype(jnp.float32)]
        )
        / 65536.0
    )


def regroup_map(matrix, devices, worker):
    line_count = matrix.shape[1] // devices
    blocks = matrix.T.reshape(devices, line_count, matrix.shape[0])
    moved = worker(lax.all_to_all(blocks, "rows", split_axis=0, concat_axis=2, tiled=True))
    return moved.reshape(line_count, moved.shape[2])


def regroup(matrix, devices):
    line_count = matrix.shape[1] // devices
    blocks = matrix.T.reshape(devices, line_count, matrix.shape[0])
    moved = lax.all_to_all(blocks, "rows", split_axis=0, concat_axis=2, tiled=True)
    return moved.reshape(line_count * moved.shape[2])


def on_device(trace_limbs, coset_shift):
    devices = lax.axis_size("rows")
    position = lax.axis_index("rows")
    values = from_limbs(trace_limbs)
    first_len = LEN_A
    second_len = LEN_B
    longer = 2 * LEN_B
    trace_len = first_len * second_len
    ext_len = 2 * trace_len
    rows_a = first_len // devices
    rows_b = second_len // devices
    rows_long = longer // devices
    back_root = pow(unity_root(trace_len), MODULUS - 2, MODULUS)
    first_back = power_table(pow(unity_root(first_len), MODULUS - 2, MODULUS), first_len // 2)
    second_back = power_table(pow(unity_root(second_len), MODULUS - 2, MODULUS), second_len // 2)
    first_fwd = power_table(unity_root(first_len), first_len // 2)
    long_fwd = power_table(unity_root(longer), longer // 2)

    def first_back_pass(block_in):
        return transform(block_in, first_back)

    def second_back_pass(block_in):
        return transform(block_in, second_back)

    def padded_pass(block_in):
        return transform(jnp.concatenate([block_in, jnp.zeros_like(block_in)], -1), first_fwd)

    def long_pass(block_in):
        return transform(block_in, long_fwd)

    matrix = values.reshape(rows_a, second_len)
    columns = regroup_map(matrix, devices, first_back_pass)
    col_ids = position * rows_b + jnp.arange(rows_b, dtype=jnp.int32)
    columns = field_mul(columns, cross_twiddle(back_root, col_ids, first_len, trace_len))
    rows_back = regroup_map(columns, devices, second_back_pass)
    inverse_len = jnp.int32(pow(trace_len, MODULUS - 2, MODULUS))
    shift_base = coset_shift[0]
    shift_first = traced_powers(
        shift_base, jnp.array([first_len], dtype=jnp.int32), first_len.bit_length()
    )[0]
    ordered = regroup(rows_back, devices).reshape(rows_b, first_len)
    inner_powers = field_mul(
        traced_powers(shift_base, jnp.arange(first_len, dtype=jnp.int32), first_len.bit_length()),
        inverse_len,
    )
    outer_powers = traced_powers(shift_first, col_ids, second_len.bit_length())
    shifted = field_mul(ordered, field_mul(outer_powers[:, None], inner_powers[None, :]))
    rows_half = first_len // (2 * devices)
    spread = regroup_map(shifted.reshape(rows_half, longer), devices, padded_pass)
    long_ids = position * rows_long + jnp.arange(rows_long, dtype=jnp.int32)
    spread = field_mul(spread, cross_twiddle(unity_root(ext_len), long_ids, first_len, ext_len))
    gathered = regroup_map(spread, devices, long_pass)
    extended = regroup(gathered, devices)
    return to_limbs(extended)


def solution(mesh):
    placed = (P(None, ("cols", "rows")), P())
    return jax.shard_map(
        on_device, mesh=mesh, in_specs=placed, out_specs=P(None, ("cols", "rows")), check_vma=False
    )
```

profile of v0, /device:TPU:2, one launch (start us, length us, event | category | flops | bytes accessed | tf_op | source)
XLA Modules:
  0.0 421.0 jit_solution(13186514072254226005)
XLA Ops:
  4.7 19.4 %all-to-all-start = ((s32[128,1,512]{2,1,0:T(1,128)}), s32[128,1,512]{2,1,0:T(1,128)S(1)}, u32[]{:S(2)}, u32[]{:S(2)}) async-start(s32[128,1,512]{2,1,0:T(1,128)} %reshape.15404), calls=%async_computation | async-start | bytes 524288 | tf_op jit(solution)/shard_map/all_to_all | solution.py:154
  79.5 4.0 compare_select_fusion.8
  84.6 16.5 %all-to-all-start.1 = ((s32[128,1,512]{2,1,0:T(1,128)}), s32[128,1,512]{2,1,0:T(1,128)S(1)}, u32[]{:S(2)}, u32[]{:S(2)}) async-start(s32[128,1,512]{2,1,0:T(1,128)} %reshape.15406), calls=%async_computation.1 | async-start | bytes 524288 | tf_op jit(solution)/shard_map/all_to_all | solution.py:154
  102.5 15.7 %all-to-all-done.1 = s32[128,1,512]{2,1,0:T(1,128)S(1)} async-done(((s32[128,1,512]{2,1,0:T(1,128)}), s32[128,1,512]{2,1,0:T(1,128)S(1)}, u32[]{:S(2)}, u32[]{:S(2)}) %all-to-all-start.1) | async-done | bytes 262176 | tf_op jit(solution)/shard_map/all_to_all | solution.py:154
  150.6 6.2 %all-to-all-start.2 = ((s32[128,1,512]{2,1,0:T(1,128)}), s32[128,1,512]{2,1,0:T(1,128)S(1)}, u32[]{:S(2)}, u32[]{:S(2)}) async-start(s32[128,1,512]{2,1,0:T(1,128)} %reshape.15408), calls=%async_computation.2 | async-start | bytes 524288 | tf_op jit(solution)/shard_map/all_to_all | solution.py:161
  156.7 3.4 broadcast_shift-right-arithmetic_fusion.2
  160.1 5.5 %fusion.2310 = (f32[64,64]{1,0:T(8,128)S(1)}, s32[64,64]{1,0:T(8,128)S(1)}) fusion(s32[64]{0:T(128)S(1)} %iota_add_fusion), kind=kLoop, calls=%fused_computation.4001 | loop fusion | flops 4603904 | bytes 33024 | tf_op jit(solution)/shard_map/convert_element_type | solution.py:19
  165.7 7.3 %all-to-all-done.2 = s32[128,1,512]{2,1,0:T(1,128)S(1)} async-done(((s32[128,1,512]{2,1,0:T(1,128)}), s32[128,1,512]{2,1,0:T(1,128)S(1)}, u32[]{:S(2)}, u32[]{:S(2)}) %all-to-all-start.2) | async-done | bytes 262176 | tf_op jit(solution)/shard_map/all_to_all | solution.py:161
  175.6 3.0 copy.642
  188.8 9.5 %all-to-all-start.3 = ((s32[128,1,512]{2,1,0:T(1,128)}), s32[128,1,512]{2,1,0:T(1,128)S(1)}, u32[]{:S(2)}, u32[]{:S(2)}) async-start(s32[128,1,512]{2,1,0:T(1,128)} %reshape.15410), calls=%async_computation.3 | async-start | bytes 524288 | tf_op jit(solution)/shard_map/all_to_all | solution.py:154
  204.2 10.2 %all-to-all-done.3 = s32[128,1,512]{2,1,0:T(1,128)S(1)} async-done(((s32[128,1,512]{2,1,0:T(1,128)}), s32[128,1,512]{2,1,0:T(1,128)S(1)}, u32[]{:S(2)}, u32[]{:S(2)}) %all-to-all-start.3) | async-done | bytes 262176 | tf_op jit(solution)/shard_map/all_to_all | solution.py:154
  217.3 5.1 %compare_select_fusion.82 = (s32[1,1,65536]{2,1,0:T(1,128)S(1)}, s32[1,1,65536]{2,1,0:T(1,128)S(1)}) fusion(s32[1,2,65536]{2,1,0:T(2,128)} %reshape_reshape.169, f32[]{:T(128)} %bitcast.99, s32[]{:T(128)} %bitcast.98, f32[]{:T(128)} %bitcast.97, s32[]{:T(128)} %bitcast.96), kind=kLoop, calls=%fused_computation.82 | loop fusion | flops 2359296 | bytes 1048592 | tf_op jit(solution)/shard_map/jit(_where)/select_n | solution.py:27
  226.5 2.9 compare_select_fusion.77
  231.1 3.0 compare_select_fusion.72
  235.8 2.9 compare_select_fusion.67
  240.4 3.0 compare_select_fusion.62
  245.1 3.2 compare_select_fusion.57
  264.1 3.0 compare_select_fusion.52
  272.4 4.5 %compare_select_fusion = s32[64,2048]{0,1:T(8,128)} fusion(s32[64,1,2,1024]{0,3,2,1:T(8,128)S(1)} %copy.716, s32[64,1,2,1024]{0,3,2,1:T(8,128)} %copy.715, s32[64,32,64]{0,2,1:T(8,128)S(1)} %get-tuple-element.193, s32[64,32,64]{0,2,1:T(8,128)S(1)} %get-tuple-element.192), kind=kLoop, calls=%fused_computation | loop fusion | flops 8257536 | bytes 2621440 | tf_op jit(solution)/shard_map/jit(_where)/select_n | solution.py:27
  279.6 6.4 %all-to-all-start.4 = ((s32[128,1,1024]{2,1,0:T(1,128)}), s32[128,1,1024]{2,1,0:T(1,128)S(1)}, u32[]{:S(2)}, u32[]{:S(2)}) async-start(s32[128,1,1024]{2,1,0:T(1,128)} %reshape.15412), calls=%async_computation.4 | async-start | bytes 1048576 | tf_op jit(solution)/shard_map/all_to_all | solution.py:154
  292.7 13.3 %all-to-all-done.4 = s32[128,1,1024]{2,1,0:T(1,128)S(1)} async-done(((s32[128,1,1024]{2,1,0:T(1,128)}), s32[128,1,1024]{2,1,0:T(1,128)S(1)}, u32[]{:S(2)}, u32[]{:S(2)}) %all-to-all-start.4) | async-done | bytes 524320 | tf_op jit(solution)/shard_map/all_to_all | solution.py:154
  311.4 4.4 %reshape_reshape.180 = s32[1,2,65536]{2,1,0:T(2,128)S(1)} reshape(s32[8192,16]{1,0:T(8,128)} %copy.676) | data formatting | bytes 1048576 | tf_op jit(solution)/shard_map/reshape;reshape | solution.py:90
  315.8 3.9 compare_select_fusion.47
  322.8 3.3 compare_select_fusion.42
  332.4 2.9 compare_select_fusion.32
  336.9 3.0 compare_select_fusion.27
  341.6 3.0 compare_select_fusion.22
  372.3 27.6 %all_to_all.81 = s32[128,1,1024]{2,1,0:T(1,128)S(1)} all-to-all(s32[128,1,1024]{2,1,0:T(1,128)S(1)} %reshape.15414), channel_id=1, replica_groups=mesh['rows'=128,'cols'=4] {'rows'}, dimensions={0} | all-to-all | bytes 1048576 | tf_op jit(solution)/shard_map/all_to_all | solution.py:161
  402.2 4.4 %copy.706 = f32[1,64,128,16]{3,2,1,0:T(8,128)} copy(f32[1,64,128,16]{1,3,2,0:T(8,128)S(1)} %get-tuple-element.139) | data formatting | bytes 1048576 | tf_op jit(solution)/shard_map/convert_element_type | solution.py:145
  406.7 3.7 convert_element_type.43681
  410.4 4.4 %copy.705 = f32[1,64,128,16]{3,2,1,0:T(8,128)} copy(f32[1,64,128,16]{1,3,2,0:T(8,128)S(1)} %get-tuple-element.138) | data formatting | bytes 1048576 | tf_op jit(solution)/shard_map/convert_element_type | solution.py:145
  414.8 3.7 convert_element_type.43677
  (535 shorter events, 199.0 us)
Async XLA Ops:
  4.7 47.4 %all-to-all-start = ((s32[128,1,512]{2,1,0:T(1,128)}), s32[128,1,512]{2,1,0:T(1,128)S(1)}, u32[]{:S(2)}, u32[]{:S(2)}) async-start(s32[128,1,512]{2,1,0:T(1,128)} %reshape.15404), calls=%async_computation | async-start | bytes 524288 | tf_op jit(solution)/shard_map/all_to_all | solution.py:154
  84.6 33.6 %all-to-all-start.1 = ((s32[128,1,512]{2,1,0:T(1,128)}), s32[128,1,512]{2,1,0:T(1,128)S(1)}, u32[]{:S(2)}, u32[]{:S(2)}) async-start(s32[128,1,512]{2,1,0:T(1,128)} %reshape.15406), calls=%async_computation.1 | async-start | bytes 524288 | tf_op jit(solution)/shard_map/all_to_all | solution.py:154
  119.7 5.5 %copy-start.6 = (f32[2]{0:T(128)S(1)}, f32[2]{0:T(128)}, u32[]{:S(2)}) copy-start(f32[2]{0:T(128)} %convert_element_type.42538) | copy-start | bytes 28
  119.7 5.5 %copy-start.7 = (f32[2]{0:T(128)S(1)}, f32[2]{0:T(128)}, u32[]{:S(2)}) copy-start(f32[2]{0:T(128)} %convert_element_type.42535) | copy-start | bytes 28
  120.5 6.0 %copy-start.4 = (f32[4]{0:T(128)S(1)}, f32[4]{0:T(128)}, u32[]{:S(2)}) copy-start(f32[4]{0:T(128)} %convert_element_type.42544) | copy-start | bytes 52
  120.6 6.0 %copy-start.5 = (f32[4]{0:T(128)S(1)}, f32[4]{0:T(128)}, u32[]{:S(2)}) copy-start(f32[4]{0:T(128)} %convert_element_type.42541) | copy-start | bytes 52
  121.2 7.7 %copy-start.3 = (f32[8]{0:T(128)S(1)}, f32[8]{0:T(128)}, u32[]{:S(2)}) copy-start(f32[8]{0:T(128)} %convert_element_type.42547) | copy-start | bytes 100
  150.6 22.4 %all-to-all-start.2 = ((s32[128,1,512]{2,1,0:T(1,128)}), s32[128,1,512]{2,1,0:T(1,128)S(1)}, u32[]{:S(2)}, u32[]{:S(2)}) async-start(s32[128,1,512]{2,1,0:T(1,128)} %reshape.15408), calls=%async_computation.2 | async-start | bytes 524288 | tf_op jit(solution)/shard_map/all_to_all | solution.py:161
  183.4 14.9 %copy-start.1 = (s32[1024]{0:T(1024)S(1)}, s32[1024]{0:T(1024)}, u32[]{:S(2)}) copy-start(s32[1024]{0:T(1024)} %reshape.15336) | copy-start | bytes 12292
  183.4 14.9 %copy-start.2 = (s32[1024]{0:T(1024)S(1)}, s32[1024]{0:T(1024)}, u32[]{:S(2)}) copy-start(s32[1024]{0:T(1024)} %reshape.15335) | copy-start | bytes 12292
  183.4 20.2 %copy-start = (s32[64,32]{0,1:T(8,128)S(1)}, s32[64,32]{0,1:T(8,128)}, u32[]{:S(2)}) copy-start(s32[64,32]{0,1:T(8,128)} %get-tuple-element.62) | copy-start | bytes 24580
  188.8 25.7 %all-to-all-start.3 = ((s32[128,1,512]{2,1,0:T(1,128)}), s32[128,1,512]{2,1,0:T(1,128)S(1)}, u32[]{:S(2)}, u32[]{:S(2)}) async-start(s32[128,1,512]{2,1,0:T(1,128)} %reshape.15410), calls=%async_computation.3 | async-start | bytes 524288 | tf_op jit(solution)/shard_map/all_to_all | solution.py:154
  279.6 26.4 %all-to-all-start.4 = ((s32[128,1,1024]{2,1,0:T(1,128)}), s32[128,1,1024]{2,1,0:T(1,128)S(1)}, u32[]{:S(2)}, u32[]{:S(2)}) async-start(s32[128,1,1024]{2,1,0:T(1,128)} %reshape.15412), calls=%async_computation.4 | async-start | bytes 1048576 | tf_op jit(solution)/shard_map/all_to_all | solution.py:154
where the time goes:
time: 427 us; the launch traced here: 421 us
  other arithmetic  165 us (39%)
  local copies, waits for them, and re-layouts  114 us (27%)
  starting transfers between devices  57.9 us (14%)
  waiting for transfers between devices  46.5 us (11%)
  blocking collectives  27.6 us (6%)
  between operations  9.93 us (2%)
    select_n x49, other arithmetic, field_add(): return jnp.where(summed < 0, summed + MODULUS, summed)  87.1 us
    all_to_all x4, starting transfers between devices, regroup_map(): lax.all_to_all(blocks, 'rows', split_axis=0, concat_axis=2, tiled=True)  51.7 us
    all_to_all x4, waiting for transfers between devices, regroup_map(): lax.all_to_all(blocks, 'rows', split_axis=0, concat_axis=2, tiled=True)  39.3 us
    all_to_all x1, blocking collectives, regroup(): lax.all_to_all(blocks, 'rows', split_axis=0, concat_axis=2, tiled=True)  27.6 us
    shift_right_arithmetic x15, other arithmetic, paired_mul(): high_part = reduce_product(factor_one >> 16, table_lifted)  18.4 us
    another operation x24, local copies, waits for them, and re-layouts, transform(): halves = leading.reshape(half_span, 2, groups * row_count)  14.8 us
    convert_element_type x92, other arithmetic, reduce_product(): field_factor.astype(jnp.float32)  12.3 us
    select_n x30, other arithmetic, field_sub(): return jnp.where(differ < 0, differ + MODULUS, differ)  11 us
  transfers between devices with their start and end apart: 5, of which 4 were waited for; matrix products, arithmetic and copies ran while one was open for 10% of the time, Pallas kernels for 0%

commit v1 on v0

v1 whole, which is shorter than its diff:
```python
import functools

import jax
import jax.numpy as jnp
import ml_dtypes
import numpy as np
from jax import lax
from jax.experimental import pallas as pl
from jax.experimental.pallas import tpu as pltpu
from jax.sharding import PartitionSpec as P

LEN_A = 2048
LEN_B = 4096
MODULUS = 2013265921
HALF = MODULUS // 2
SPLIT = 15
LIMBS = 4
BYTE_BIAS = -2139062144

TRACE_LEN = LEN_A * LEN_B
EXT_LEN = 2 * TRACE_LEN
GROUP = 128
SIDE = 256
LONG = 2 * SIDE
LOCAL = SIDE * SIDE
LANES = 128


def unity_root(length):
    return pow(pow(31, 15, MODULUS), (1 << 27) // length, MODULUS)


BACK_ROOT = pow(unity_root(TRACE_LEN), MODULUS - 2, MODULUS)
FWD_ROOT = unity_root(EXT_LEN)


def powers_of(base, exponents):
    exponents = np.asarray(exponents, dtype=np.int64)
    result = np.ones(exponents.shape, dtype=np.int64)
    square = base % MODULUS
    for bit in range(int(exponents.max(initial=0)).bit_length()):
        result = np.where(exponents >> bit & 1 == 1, mul_mod(result, square), result)
        square = square * square % MODULUS
    return result


def mul_mod(left, right):
    return left * right % MODULUS


def centered(values):
    values = values % MODULUS
    return np.where(values > HALF, values - MODULUS, values)


def both_halves(values):
    return np.stack([centered(values), centered(mul_mod(values, 1 << SPLIT))]).astype(np.int32)


def limbs_of(values):
    rest = centered(values)
    digits = []
    for _ in range(LIMBS):
        digit = (rest + 128) % 256 - 128
        digits.append(digit)
        rest = (rest - digit) // 256
    return np.stack(digits)


def limb_matrix(matrix):
    blocks = np.stack([limbs_of(mul_mod(matrix, 256**a)) for a in range(LIMBS)], axis=2)
    out_len, in_len = matrix.shape
    return np.ascontiguousarray(
        blocks.reshape(LIMBS * out_len, LIMBS * in_len).astype(ml_dtypes.bfloat16)
    )


def dft_matrix(root, out_len, in_len):
    return powers_of(root, np.arange(out_len)[:, None] * np.arange(in_len)[None, :])


SPLIT_OUT = 2
MATRIX_ROWS = 3 * LIMBS * SIDE
TABLE_ROWS = 4096
LINE_ROWS = 16
LINES_AT = 1024


def in_parts(matrix, count):
    rows, cols = matrix.shape
    parts = matrix.reshape(LIMBS, SPLIT_OUT, count // SPLIT_OUT, cols).transpose(1, 0, 2, 3)
    return parts.reshape(rows, cols)


@functools.cache
def tables():
    lines = np.arange(GROUP)
    side = np.arange(SIDE)
    long = np.arange(LONG)
    tile = np.arange(LOCAL // GROUP)
    root_side = unity_root(SIDE)
    back_side = pow(root_side, MODULUS - 2, MODULUS)
    root_group = unity_root(GROUP)
    back_group = pow(root_group, MODULUS - 2, MODULUS)
    back_local = pow(unity_root(LOCAL), MODULUS - 2, MODULUS)
    side_back = limb_matrix(dft_matrix(back_side, SIDE, SIDE))
    wide = LIMBS * SIDE
    matrices = np.zeros((MATRIX_ROWS, 2 * wide), ml_dtypes.bfloat16)
    matrices[:wide] = in_parts(limb_matrix(dft_matrix(unity_root(LONG), LONG, SIDE)), LONG).T
    matrices[wide : 2 * wide, :wide] = in_parts(side_back, SIDE)
    matrices[wide : 2 * wide, wide:] = limb_matrix(dft_matrix(root_side, SIDE, SIDE))
    small = LIMBS * GROUP
    matrices[2 * wide :, :small] = np.concatenate(
        [limb_matrix(dft_matrix(root, GROUP, GROUP)) for root in (back_group, root_group)]
    )

    powers = np.zeros((TABLE_ROWS, LONG), np.int32)
    powers[0:512] = both_halves(
        powers_of(unity_root(2 * LOCAL), side[:, None] * long[None, :])
    ).reshape(512, LONG)
    powers[512:768] = np.concatenate(
        both_halves(powers_of(back_local, side[:, None] * side[None, :])), axis=1
    )
    powers[768:1024] = both_halves(
        powers_of(BACK_ROOT, lines[:, None] * tile[None, :])
    ).reshape(256, LONG)
    own = np.zeros((GROUP, LINE_ROWS, LONG), np.int32)

    def place_pair(root, exponents, row, lane):
        pair = both_halves(powers_of(root, lines[:, None] * exponents[None, :]))
        own[:, row : row + 2, lane : lane + exponents.size] = pair.transpose(1, 0, 2)

    place_pair(FWD_ROOT, long, 0, 0)
    place_pair(FWD_ROOT, LONG * side, 8, 0)
    place_pair(BACK_ROOT, tile.size * lines, 8, SIDE)
    powers[LINES_AT : LINES_AT + GROUP * LINE_ROWS] = own.reshape(GROUP * LINE_ROWS, LONG)
    return matrices, powers


def times_modulus(count):
    return (count << 31) - (count << 27) + count


def toward_zero(value):
    return value.astype(jnp.int32)


def to_nearest(value):
    return jnp.floor(value + 0.5).astype(jnp.int32)


def paired_mul(value, plain, lifted, whole=toward_zero):
    high = value >> SPLIT
    low = value & ((1 << SPLIT) - 1)
    scale = np.float32(1.0 / MODULUS)
    estimate = high.astype(jnp.float32) * (lifted.astype(jnp.float32) * scale) + low.astype(
        jnp.float32
    ) * (plain.astype(jnp.float32) * scale)
    return high * lifted + low * plain - times_modulus(whole(estimate))


near_mul = functools.partial(paired_mul, whole=to_nearest)


def lift(value):
    once, twice = (int(centered(np.int64(1 << k * SPLIT))) for k in (1, 2))
    return near_mul(value, jnp.int32(once), jnp.int32(twice))


def digits(value, axis):
    biased = (value + jnp.int32(BYTE_BIAS)) ^ jnp.int32(BYTE_BIAS)
    parts = [(biased << (24 - 8 * k)) >> 24 for k in range(LIMBS - 1)] + [biased >> 24]
    return jnp.concatenate([part.astype(jnp.float32).astype(jnp.bfloat16) for part in parts], axis)


def combine(part0, part1, part2, part3):
    estimate = (
        part3 * np.float32(2.0**24 / MODULUS)
        + part2 * np.float32(2.0**16 / MODULUS)
        + part1 * np.float32(2.0**8 / MODULUS)
    )
    whole = [part.astype(jnp.int32) for part in (part0, part1, part2, part3)]
    total = whole[0] + (whole[1] << 8) + (whole[2] << 16) + (whole[3] << 24)
    return total - times_modulus(toward_zero(estimate))


def dot(left, right):
    return jnp.dot(left, right, preferred_element_type=jnp.float32)


def from_rows(result, count):
    return combine(*(result[k * count : (k + 1) * count] for k in range(LIMBS)))


def from_cols(result, count):
    return combine(*(result[:, k * count : (k + 1) * count] for k in range(LIMBS)))


def load(sources, targets, sems):
    copies = [
        pltpu.make_async_copy(source, target, sems.at[k])
        for k, (source, target) in enumerate(zip(sources, targets, strict=True))
    ]
    for copy in copies:
        copy.start()
    return copies


def as_column(line):
    return jnp.concatenate(
        [
            jnp.broadcast_to(line[:, k : k + LANES], (LANES, LANES)).T
            for k in range(0, line.shape[1], LANES)
        ],
        0,
    )


def own_rows(place):
    return pl.ds(pl.multiple_of(LINES_AT + place * LINE_ROWS, LINE_ROWS), LINE_ROWS)


def join_kernel(limbs_ref, out_ref):
    rows = out_ref.shape[0]
    low = (limbs_ref[pl.ds(0, rows, stride=2), :] * 65536.0).astype(jnp.int32)
    high = (limbs_ref[pl.ds(1, rows, stride=2), :] * 65536.0).astype(jnp.int32)
    joined = (high << 16) + low
    out_ref[...] = jnp.where(joined > HALF, joined - MODULUS, joined)


def table_kernel(
    place_ref, shift_ref, powers_hbm, out_hbm, own_ref, shift_table_ref, ext_ref, sems
):
    place = place_ref[0]
    own = load([powers_hbm.at[own_rows(place)]], [own_ref], sems.at[pl.ds(0, 1)])

    first = jnp.full((8, LANES), shift_ref[0], jnp.int32)
    square = jnp.where(first > HALF, first - MODULUS, first)
    inverse_len = int(centered(np.int64(pow(TRACE_LEN, MODULUS - 2, MODULUS))))
    factor = jnp.full((8, LANES), inverse_len, jnp.int32)
    rows = lax.broadcasted_iota(jnp.int32, (SIDE, LANES), 0)
    column = jnp.ones((SIDE, LANES), jnp.int32)
    cols = lax.broadcasted_iota(jnp.int32, (8, SIDE), 1)
    line = None
    for bit in range(23):
        lifted = lift(square)
        if bit < 7:
            factor = jnp.where(place >> bit & 1 == 1, near_mul(factor, square, lifted), factor)
        elif bit < 15:
            plain_row, lifted_row = square[0:1], lifted[0:1]
            column = jnp.where(
                rows >> (bit - 7) & 1 == 1, near_mul(column, plain_row, lifted_row), column
            )
        else:
            if line is None:
                line = jnp.concatenate([factor] * (SIDE // LANES), 1)
            plain_row = jnp.concatenate([square] * (SIDE // LANES), 1)
            lifted_row = jnp.concatenate([lifted] * (SIDE // LANES), 1)
            line = jnp.where(
                cols >> (bit - 15) & 1 == 1, near_mul(line, plain_row, lifted_row), line
            )
        square = near_mul(square, square, lifted)
    line_lifted = lift(line)
    for k in range(SIDE // LANES):
        cols = slice(k * LANES, (k + 1) * LANES)
        value = near_mul(column, line[0:1, cols], line_lifted[0:1, cols])
        shift_table_ref[:, cols] = value
        shift_table_ref[:, SIDE + k * LANES : SIDE + (k + 1) * LANES] = lift(value)
    stores = load(
        [shift_table_ref], [out_hbm.at[pl.ds(2 * SIDE, SIDE)]], sems.at[pl.ds(1, 1)]
    )

    own[0].wait()
    column = as_column(own_ref[8:9, 0:SIDE])
    for k in range(LONG // LANES):
        cols = slice(k * LANES, (k + 1) * LANES)
        value = near_mul(column, own_ref[0:1, cols], own_ref[1:2, cols])
        ext_ref[0:SIDE, cols] = value
        ext_ref[SIDE:, cols] = lift(value)
    stores += load([ext_ref], [out_hbm.at[pl.ds(0, 2 * SIDE)]], sems.at[pl.ds(2, 1)])
    for copy in stores:
        copy.wait()


def gather_rows(ref, lines, per_line):
    return jnp.concatenate(
        [ref[pl.ds(k, lines, stride=per_line), :] for k in range(per_line)], 1
    )


def scatter_rows(ref, value, per_line, first=0):
    lines = value.shape[0]
    for k in range(value.shape[1] // LANES):
        ref[pl.ds(first + k, lines, stride=per_line), :] = value[:, k * LANES : (k + 1) * LANES]


def group_matrix(matrices_hbm, index):
    size = LIMBS * GROUP
    return matrices_hbm.at[pl.ds(2 * LIMBS * SIDE + index * size, size), pl.ds(0, size)]


def group_products(in_ref, matrix_ref, ready, finish):
    per_line = in_ref.shape[0] // GROUP
    step = 2
    splits = [
        digits(
            jnp.concatenate(
                [in_ref[pl.ds(first + k, GROUP, stride=per_line), :] for k in range(step)], 1
            ),
            0,
        )
        for first in range(0, per_line, step)
    ]
    ready()
    last = None
    for index, split in enumerate(splits):
        result = dot(matrix_ref[...], split)
        if last is not None:
            finish((index - 1) * step, from_rows(last, GROUP))
        last = result
    finish((len(splits) - 1) * step, from_rows(last, GROUP))


def group_back_kernel(
    place_ref,
    in_ref,
    matrices_hbm,
    powers_hbm,
    made_hbm,
    out_ref,
    matrix_ref,
    own_ref,
    base_ref,
    sems,
):
    copies = load(
        [
            group_matrix(matrices_hbm, 0),
            powers_hbm.at[own_rows(place_ref[0])],
            powers_hbm.at[pl.ds(768, 2 * GROUP)],
        ],
        [matrix_ref, own_ref, base_ref],
        sems,
    )
    columns = []

    def ready():
        for copy in copies:
            copy.wait()
        for row in (8, 9):
            column = as_column(own_ref[row : row + 1, SIDE : SIDE + LANES])
            columns.append(jnp.concatenate([column, column], 1))

    def finish(first, value):
        cols = slice(first * LANES, first * LANES + value.shape[1])
        value = paired_mul(value, base_ref[0:GROUP, cols], base_ref[GROUP:, cols])
        value = paired_mul(value, *columns)
        scatter_rows(out_ref, value, in_ref.shape[0] // GROUP, first)

    group_products(in_ref, matrix_ref, ready, finish)


def group_fwd_kernel(in_ref, matrices_hbm, out_ref, matrix_ref, sems):
    copies = load([group_matrix(matrices_hbm, 1)], [matrix_ref], sems)

    def finish(first, value):
        value = jnp.where(value < 0, value + MODULUS, value)
        value = jnp.where(value >= MODULUS, value - MODULUS, value)
        value = jnp.where(value < 0, value + MODULUS, value)
        scatter_rows(out_ref, value, in_ref.shape[0] // GROUP, first)

    group_products(in_ref, matrix_ref, copies[0].wait, finish)


def middle_kernel(
    in_ref,
    matrices_hbm,
    powers_hbm,
    made_hbm,
    out_ref,
    side_back_ref,
    mid_back_ref,
    shift_ref,
    long_fwd_t_ref,
    mid_fwd_ref,
    side_fwd_ref,
    ext_ref,
    sems,
):
    wide = LIMBS * SIDE
    part = wide // SPLIT_OUT
    rows = SIDE // SPLIT_OUT
    cols = LONG // SPLIT_OUT
    back = (((1,), (1,)), ((), ()))
    copies = load(
        [
            matrices_hbm.at[pl.ds(wide, wide), pl.ds(0, wide)],
            powers_hbm.at[pl.ds(2 * SIDE, SIDE)],
            made_hbm.at[pl.ds(2 * SIDE, SIDE)],
            matrices_hbm.at[pl.ds(0, wide)],
            powers_hbm.at[pl.ds(0, 2 * SIDE)],
            matrices_hbm.at[pl.ds(wide, wide), pl.ds(wide, wide)],
            made_hbm.at[pl.ds(0, 2 * SIDE)],
        ],
        [
            side_back_ref,
            mid_back_ref,
            shift_ref,
            long_fwd_t_ref,
            mid_fwd_ref,
            side_fwd_ref,
            ext_ref,
        ],
        sems,
    )

    def first(k, split):
        return dot(side_back_ref[k * part : (k + 1) * part, :], split)

    def after_first(k, result):
        here = slice(k * rows, (k + 1) * rows)
        result = from_rows(result, rows)
        return digits(
            paired_mul(result, mid_back_ref[here, 0:SIDE], mid_back_ref[here, SIDE:]), 1
        )

    def second(split):
        return lax.dot_general(
            split, side_back_ref[...], back, preferred_element_type=jnp.float32
        )

    def after_second(k, result):
        here = slice(k * rows, (k + 1) * rows)
        half = SIDE // SPLIT_OUT
        result = jnp.concatenate(
            [from_cols(result[:, n * part : (n + 1) * part], half) for n in range(SPLIT_OUT)], 1
        )
        return digits(paired_mul(result, shift_ref[here, 0:SIDE], shift_ref[here, SIDE:]), 1)

    split = digits(gather_rows(in_ref, SIDE, SIDE // LANES), 0)
    for copy in copies[:3]:
        copy.wait()
    one = first(0, split)
    two = first(1, split)
    one = second(after_first(0, one))
    two = second(after_first(1, two))
    one = after_second(0, one)
    two = after_second(1, two)
    split = jnp.concatenate([one, two], 0)
    for copy in copies[3:]:
        copy.wait()

    def third(k):
        return dot(split, long_fwd_t_ref[:, k * wide : (k + 1) * wide])

    def after_third(k, result):
        here = slice(k * cols, (k + 1) * cols)
        result = from_cols(result, cols)
        return digits(paired_mul(result, mid_fwd_ref[0:SIDE, here], mid_fwd_ref[SIDE:, here]), 0)

    def fourth(split):
        return dot(side_fwd_ref[...], split)

    def after_fourth(k, result):
        here = slice(k * cols, (k + 1) * cols)
        result = from_rows(result, SIDE)
        result = paired_mul(result, ext_ref[0:SIDE, here], ext_ref[SIDE:, here])
        scatter_rows(out_ref, result, LONG // LANES, k * cols // LANES)

    one = third(0)
    two = third(1)
    one = fourth(after_third(0, one))
    two = fourth(after_third(1, two))
    after_fourth(0, one)
    after_fourth(1, two)


def limbs_kernel(in_ref, out_ref):
    value = in_ref[...]
    rows = in_ref.shape[0]
    scale = np.float32(1.0 / 65536.0)
    out_ref[pl.ds(0, rows, stride=2), :] = (value & 65535).astype(jnp.float32) * scale
    out_ref[pl.ds(1, rows, stride=2), :] = (value >> 16).astype(jnp.float32) * scale


def exchange(rows):
    blocks = rows.reshape(GROUP, rows.shape[0] // GROUP, LANES)
    moved = lax.all_to_all(blocks, "rows", split_axis=0, concat_axis=0, tiled=True)
    return moved.reshape(rows.shape)


def on_device(trace_limbs, coset_shift):
    matrices, powers = (jnp.asarray(table) for table in tables())
    place = lax.axis_index("rows").astype(jnp.int32).reshape(1)
    rows = LOCAL // LANES
    wide = LIMBS * SIDE
    smem = pl.BlockSpec(memory_space=pltpu.SMEM)
    vmem = pl.BlockSpec(memory_space=pltpu.VMEM)
    anywhere = pl.BlockSpec(memory_space=pl.ANY)

    def ints(*shape):
        return jax.ShapeDtypeStruct(shape, jnp.int32)

    def limb(*shape):
        return jax.ShapeDtypeStruct(shape, jnp.bfloat16)

    def call(name, body, out_shape, in_specs, scratch=(), sems=0, cost=1, out_spec=vmem):
        scratch = [pltpu.VMEM(a.shape, a.dtype) for a in scratch]
        if sems:
            scratch.append(pltpu.SemaphoreType.DMA((sems,)))
        return pl.pallas_call(
            body,
            out_shape=out_shape,
            in_specs=in_specs,
            out_specs=out_spec,
            scratch_shapes=scratch,
            compiler_params=pltpu.CompilerParams(vmem_limit_bytes=48 << 20),
            cost_estimate=pl.CostEstimate(
                flops=cost * 1_000_000, bytes_accessed=1 << 20, transcendentals=0
            ),
            name=name,
        )

    limbs = trace_limbs.reshape(2, rows, LANES).transpose(1, 0, 2).reshape(2 * rows, LANES)
    values = call("join_limbs", join_kernel, ints(rows, LANES), [vmem])(limbs)
    made = call(
        "power_tables",
        table_kernel,
        ints(TABLE_ROWS, LONG),
        [smem, smem, anywhere],
        [ints(LINE_ROWS, LONG), ints(SIDE, LONG), ints(2 * SIDE, LONG)],
        3,
        300,
        anywhere,
    )(place, coset_shift, powers)
    columns = exchange(values)
    columns = call(
        "group_back",
        group_back_kernel,
        ints(rows, LANES),
        [smem, vmem, anywhere, anywhere, anywhere],
        [limb(LIMBS * GROUP, LIMBS * GROUP), ints(LINE_ROWS, LONG), ints(2 * GROUP, LONG)],
        3,
        300,
    )(place, columns, matrices, powers, made)
    block = exchange(columns)
    extended = call(
        "block_transforms",
        middle_kernel,
        ints(2 * rows, LANES),
        [vmem, anywhere, anywhere, anywhere],
        [
            limb(wide, wide),
            ints(SIDE, LONG),
            ints(SIDE, LONG),
            limb(wide, 2 * wide),
            ints(2 * SIDE, LONG),
            limb(wide, wide),
            ints(2 * SIDE, LONG),
        ],
        7,
        4000,
    )(block, matrices, powers, made)
    columns = exchange(extended)
    columns = call(
        "group_fwd",
        group_fwd_kernel,
        ints(2 * rows, LANES),
        [vmem, anywhere],
        [limb(LIMBS * GROUP, LIMBS * GROUP)],
        1,
        500,
    )(columns, matrices)
    ordered = exchange(columns)
    pairs = call(
        "split_limbs", limbs_kernel, jax.ShapeDtypeStruct((4 * rows, LANES), jnp.float32), [vmem]
    )(ordered)
    return pairs.reshape(2 * rows, 2, LANES).transpose(1, 0, 2).reshape(2, 2 * rows * LANES)


def solution(mesh):
    placed = (P(None, ("cols", "rows")), P())
    return jax.shard_map(
        on_device, mesh=mesh, in_specs=placed, out_specs=P(None, ("cols", "rows")), check_vma=False
    )
```

time: 427 us -> 128 us (0.30); the launches traced: 421 us -> 127 us
  other arithmetic: 165 us -> 0 us
  local copies, waits for them, and re-layouts: 114 us -> 1.04 us
  blocking collectives: 27.6 us -> 75.3 us
  starting transfers between devices: 57.9 us -> 19.4 us
  waiting for transfers between devices: 46.5 us -> 13.6 us
  Pallas kernels: 0 us -> 17.4 us
  between operations: 9.93 us -> 0.7 us
    select_n x79 -> x0, other arithmetic: 98.1 us -> none  [the longest x49 87.1 us: field_add(): return jnp.where(summed < 0, summed + MODULUS, summed)]
    all_to_all x1 -> x3, blocking collectives: 27.6 us -> 75.3 us  [exchange(): lax.all_to_all(blocks, 'rows', split_axis=0, concat_axis=0, tiled=True)]
    all_to_all x5 -> x1, starting transfers between devices: 57.9 us -> 19.4 us  [exchange(): lax.all_to_all(blocks, 'rows', split_axis=0, concat_axis=0, tiled=True)]
    another operation x82 -> x0, local copies, waits for them, and re-layouts: 36.8 us -> none  [the longest x24 14.8 us: transform(): halves = leading.reshape(half_span, 2, groups * row_count)]
    all_to_all x5 -> x1, waiting for transfers between devices: 46.5 us -> 13.6 us  [exchange(): lax.all_to_all(blocks, 'rows', split_axis=0, concat_axis=0, tiled=True)]
    shift_right_arithmetic x25 -> x0, other arithmetic: 28.7 us -> none  [the longest x15 18.4 us: paired_mul(): high_part = reduce_product(factor_one >> 16, table_lifted)]
    pallas_call x0 -> x6, Pallas kernels: none -> 17.4 us  [the longest x1 7.86 us: on_device(): call('block_transforms', middle_kernel, ints(2 * rows, LANES), [vmem, any...]
    convert_element_type x6 -> x0, local copies, waits for them, and re-layouts: 16.4 us -> none  [the longest x2 8.11 us: to_limbs(): (field_values >> 16).astype(jnp.float32)]
  transfers between devices with their start and end apart: 5 -> 1, of which waited for: 4 -> 1; matrix products, arithmetic and copies ran while one was open for 10% -> 0% of each run, Pallas kernels for 0% -> 3%
where the time goes in v1:
time: 128 us; the launch traced here: 127 us
  blocking collectives  75.3 us (59%)
  starting transfers between devices  19.4 us (15%)
  Pallas kernels  17.4 us (14%)
  waiting for transfers between devices  13.6 us (11%)
    all_to_all x3, blocking collectives, exchange(): lax.all_to_all(blocks, 'rows', split_axis=0, concat_axis=0, tiled=True)  75.3 us
    all_to_all x1, starting transfers between devices, exchange(): lax.all_to_all(blocks, 'rows', split_axis=0, concat_axis=0, tiled=True)  19.4 us
    all_to_all x1, waiting for transfers between devices, exchange(): lax.all_to_all(blocks, 'rows', split_axis=0, concat_axis=0, tiled=True)  13.6 us
    pallas_call x1, Pallas kernels, on_device(): call('block_transforms', middle_kernel, ints(2 * rows, LANES), [vmem, any...  7.86 us
    pallas_call x1, Pallas kernels, on_device(): call('power_tables', table_kernel, ints(TABLE_ROWS, LONG), [smem, smem, a...  3.43 us
  transfers between devices with their start and end apart: 1, of which 1 were waited for; matrix products, arithmetic and copies ran while one was open for 0% of the time, Pallas kernels for 3%

profile of v1, /device:TPU:2, one launch (start us, length us, event | category | flops | bytes accessed | tf_op | source)
XLA Modules:
  0.0 127.4 jit_solution(11228530933070631551)
XLA Ops:
  0.0 0.0 copy-start
  0.0 1.0 copy-done
  1.0 0.8 join_limbs.1
  1.8 19.4 %all-to-all-start = ((s32[128,4,128]{2,1,0:T(4,128)}), s32[128,4,128]{2,1,0:T(4,128)S(1)}, u32[]{:S(2)}, u32[]{:S(2)}) async-start(s32[128,4,128]{2,1,0:T(4,128)} %bitcast.4), calls=%async_computation | async-start | bytes 524288 | tf_op jit(solution)/shard_map/all_to_all | solution.py:488
  21.9 3.4 %power_tables.1.made_hbm = s32[4096,512]{1,0:T(8,128)} custom-call(s32[1]{0:T(128)} %bitcast.place_ref, s32[1]{0:T(128)S(6)} %copy.7.shift_ref, s32[4096,512]{1,0:T(8,128)} %constant.11.clone.powers_hbm), custom_call_target="tpu_custom_call" | custom-call | flops 300000000 | bytes 1048576 | tf_op jit(solution)/shard_map/power_tables/pallas_call | solution.py:526
  25.3 13.6 %all-to-all-done = s32[128,4,128]{2,1,0:T(4,128)S(1)} async-done(((s32[128,4,128]{2,1,0:T(4,128)}), s32[128,4,128]{2,1,0:T(4,128)S(1)}, u32[]{:S(2)}, u32[]{:S(2)}) %all-to-all-start) | async-done | bytes 262176 | tf_op jit(solution)/shard_map/all_to_all | solution.py:488
  38.9 2.1 %group_back.1 = s32[512,128]{1,0:T(8,128)S(1)} custom-call(s32[1]{0:T(128)} %bitcast.place_ref, s32[512,128]{1,0:T(8,128)S(1)} %bitcast.23, bf16[3072,2048]{1,0:T(8,128)(2,1)} %constant.10.clone.matrices_hbm, s32[4096,512]{1,0:T(8,128)} %constant.11.clone.powers_hbm, s32[4096,512]{1,0:T(8,128)} %power_tables.1.made_hbm), custom_call_target="tpu_custom_call" | custom-call | flops 300000000 | bytes 1048576 | tf_op jit(solution)/shard_map/group_back/pallas_call | solution.py:537
  41.0 21.9 %all_to_all.20 = s32[128,4,128]{2,1,0:T(4,128)S(1)} all-to-all(s32[128,4,128]{2,1,0:T(4,128)S(1)} %bitcast.25), channel_id=1, replica_groups=mesh['rows'=128,'cols'=4] {'rows'}, dimensions={0} | all-to-all | bytes 524288 | tf_op jit(solution)/shard_map/all_to_all | solution.py:488
  62.9 7.9 %block_transforms.1 = s32[1024,128]{1,0:T(8,128)S(1)} custom-call(s32[512,128]{1,0:T(8,128)S(1)} %bitcast.24, bf16[3072,2048]{1,0:T(8,128)(2,1)} %constant.10.clone.matrices_hbm, s32[4096,512]{1,0:T(8,128)} %constant.11.clone.powers_hbm, s32[4096,512]{1,0:T(8,128)} %power_tables.1.made_hbm), custom_call_target="tpu_custom_call" | custom-call | flops 4000000000 | bytes 1048576 | tf_op jit(solution)/shard_map/block_transforms/pallas_call | solution.py:547
  70.7 26.0 %all_to_all.21 = s32[128,8,128]{2,1,0:T(8,128)S(1)} all-to-all(s32[128,8,128]{2,1,0:T(8,128)S(1)} %bitcast.19), channel_id=1, replica_groups=mesh['rows'=128,'cols'=4] {'rows'}, dimensions={0} | all-to-all | bytes 1048576 | tf_op jit(solution)/shard_map/all_to_all | solution.py:488
  96.7 2.1 %group_fwd.1 = s32[1024,128]{1,0:T(8,128)S(1)} custom-call(s32[1024,128]{1,0:T(8,128)S(1)} %bitcast.21, bf16[3072,2048]{1,0:T(8,128)(2,1)} %constant.10.clone.matrices_hbm), custom_call_target="tpu_custom_call" | custom-call | flops 500000000 | bytes 1048576 | tf_op jit(solution)/shard_map/group_fwd/pallas_call | solution.py:565
  98.8 27.4 %all_to_all.22 = s32[128,8,128]{2,1,0:T(8,128)S(1)} all-to-all(s32[128,8,128]{2,1,0:T(8,128)S(1)} %bitcast.22), channel_id=1, replica_groups=mesh['rows'=128,'cols'=4] {'rows'}, dimensions={0} | all-to-all | bytes 1048576 | tf_op jit(solution)/shard_map/all_to_all | solution.py:488
  126.3 1.1 split_limbs.1
Async XLA Ops:
  0.0 1.0 copy-start
  1.8 37.0 %all-to-all-start = ((s32[128,4,128]{2,1,0:T(4,128)}), s32[128,4,128]{2,1,0:T(4,128)S(1)}, u32[]{:S(2)}, u32[]{:S(2)}) async-start(s32[128,4,128]{2,1,0:T(4,128)} %bitcast.4), calls=%async_computation | async-start | bytes 524288 | tf_op jit(solution)/shard_map/all_to_all | solution.py:488

commit v2 on v1

--- a/solution.py
+++ b/solution.py
@@ -80,7 +80,7 @@
 
 
 SPLIT_OUT = 2
-MATRIX_ROWS = 3 * LIMBS * SIDE
+MATRIX_ROWS = 4 * LIMBS * SIDE + LIMBS * GROUP
 TABLE_ROWS = 4096
 LINE_ROWS = 16
 LINES_AT = 1024
@@ -98,20 +98,20 @@
     side = np.arange(SIDE)
     long = np.arange(LONG)
     tile = np.arange(LOCAL // GROUP)
-    root_side = unity_root(SIDE)
-    back_side = pow(root_side, MODULUS - 2, MODULUS)
+    back_side = pow(unity_root(SIDE), MODULUS - 2, MODULUS)
     root_group = unity_root(GROUP)
     back_group = pow(root_group, MODULUS - 2, MODULUS)
     back_local = pow(unity_root(LOCAL), MODULUS - 2, MODULUS)
     side_back = limb_matrix(dft_matrix(back_side, SIDE, SIDE))
     wide = LIMBS * SIDE
-    matrices = np.zeros((MATRIX_ROWS, 2 * wide), ml_dtypes.bfloat16)
-    matrices[:wide] = in_parts(limb_matrix(dft_matrix(unity_root(LONG), LONG, SIDE)), LONG).T
-    matrices[wide : 2 * wide, :wide] = in_parts(side_back, SIDE)
-    matrices[wide : 2 * wide, wide:] = limb_matrix(dft_matrix(root_side, SIDE, SIDE))
-    small = LIMBS * GROUP
-    matrices[2 * wide :, :small] = np.concatenate(
-        [limb_matrix(dft_matrix(root, GROUP, GROUP)) for root in (back_group, root_group)]
+    matrices = np.zeros((MATRIX_ROWS, wide), ml_dtypes.bfloat16)
+    long_fwd = in_parts(limb_matrix(dft_matrix(unity_root(LONG), LONG, SIDE)), LONG)
+    matrices[:wide] = long_fwd[:wide].T
+    matrices[wide : 2 * wide] = long_fwd[wide:].T
+    matrices[2 * wide : 3 * wide] = in_parts(side_back, SIDE)
+    matrices[3 * wide : 4 * wide] = side_back.T
+    matrices[4 * wide :] = np.concatenate(
+        [limb_matrix(dft_matrix(root, GROUP, GROUP)) for root in (back_group, root_group)], axis=1
     )
 
     powers = np.zeros((TABLE_ROWS, LONG), np.int32)
@@ -131,14 +131,10 @@
         own[:, row : row + 2, lane : lane + exponents.size] = pair.transpose(1, 0, 2)
 
     place_pair(FWD_ROOT, long, 0, 0)
-    place_pair(FWD_ROOT, LONG * side, 8, 0)
+    place_pair(FWD_ROOT, LONG * (-side % SIDE), 8, 0)
     place_pair(BACK_ROOT, tile.size * lines, 8, SIDE)
     powers[LINES_AT : LINES_AT + GROUP * LINE_ROWS] = own.reshape(GROUP * LINE_ROWS, LONG)
     return matrices, powers
-
-
-def times_modulus(count):
-    return (count << 31) - (count << 27) + count
 
 
 def toward_zero(value):
@@ -153,10 +149,9 @@
     high = value >> SPLIT
     low = value & ((1 << SPLIT) - 1)
     scale = np.float32(1.0 / MODULUS)
-    estimate = high.astype(jnp.float32) * (lifted.astype(jnp.float32) * scale) + low.astype(
-        jnp.float32
-    ) * (plain.astype(jnp.float32) * scale)
-    return high * lifted + low * plain - times_modulus(whole(estimate))
+    upper = high.astype(jnp.float32) * lifted.astype(jnp.float32)
+    lower = low.astype(jnp.float32) * plain.astype(jnp.float32)
+    return high * lifted + low * plain - whole((upper + lower) * scale) * MODULUS
 
 
 near_mul = functools.partial(paired_mul, whole=to_nearest)
@@ -181,7 +176,7 @@
     )
     whole = [part.astype(jnp.int32) for part in (part0, part1, part2, part3)]
     total = whole[0] + (whole[1] << 8) + (whole[2] << 16) + (whole[3] << 24)
-    return total - times_modulus(toward_zero(estimate))
+    return total - toward_zero(estimate) * MODULUS
 
 
 def dot(left, right):
@@ -220,12 +215,22 @@
     return pl.ds(pl.multiple_of(LINES_AT + place * LINE_ROWS, LINE_ROWS), LINE_ROWS)
 
 
-def join_kernel(limbs_ref, out_ref):
-    rows = out_ref.shape[0]
-    low = (limbs_ref[pl.ds(0, rows, stride=2), :] * 65536.0).astype(jnp.int32)
-    high = (limbs_ref[pl.ds(1, rows, stride=2), :] * 65536.0).astype(jnp.int32)
-    joined = (high << 16) + low
-    out_ref[...] = jnp.where(joined > HALF, joined - MODULUS, joined)
+def join_kernel(limbs_hbm, out_hbm, limbs_ref, out_ref, in_sems, out_sems):
+    parts = in_sems.shape[0]
+    rows = out_ref.shape[0] // parts
+    pairs = [pl.ds(2 * rows * k, 2 * rows) for k in range(parts)]
+    lines = [pl.ds(rows * k, rows) for k in range(parts)]
+    copies = load([limbs_hbm.at[r] for r in pairs], [limbs_ref.at[r] for r in pairs], in_sems)
+    stores = []
+    for k, copy in enumerate(copies):
+        copy.wait()
+        low = limbs_ref[pl.ds(2 * rows * k, rows, stride=2), :] * 65536.0
+        high = limbs_ref[pl.ds(2 * rows * k + 1, rows, stride=2), :] * 65536.0
+        joined = (high.astype(jnp.int32) << 16) + low.astype(jnp.int32)
+        out_ref[lines[k], :] = jnp.where(joined > HALF, joined - MODULUS, joined)
+        stores += load([out_ref.at[lines[k]]], [out_hbm.at[lines[k]]], out_sems.at[pl.ds(k, 1)])
+    for copy in stores:
+        copy.wait()
 
 
 def table_kernel(
@@ -296,7 +301,7 @@
 
 def group_matrix(matrices_hbm, index):
     size = LIMBS * GROUP
-    return matrices_hbm.at[pl.ds(2 * LIMBS * SIDE + index * size, size), pl.ds(0, size)]
+    return matrices_hbm.at[pl.ds(4 * LIMBS * SIDE, size), pl.ds(index * size, size)]
 
 
 def group_products(in_ref, matrix_ref, ready, finish):
@@ -328,10 +333,14 @@
     powers_hbm,
     made_hbm,
     out_ref,
+    side_back_ref,
+    mid_back_ref,
+    shift_ref,
     matrix_ref,
     own_ref,
     base_ref,
     sems,
+    next_sems,
 ):
     copies = load(
         [
@@ -342,6 +351,15 @@
         [matrix_ref, own_ref, base_ref],
         sems,
     )
+    brought = load(
+        [
+            matrices_hbm.at[pl.ds(2 * LIMBS * SIDE, LIMBS * SIDE)],
+            powers_hbm.at[pl.ds(2 * SIDE, SIDE)],
+            made_hbm.at[pl.ds(2 * SIDE, SIDE)],
+        ],
+        [side_back_ref, mid_back_ref, shift_ref],
+        next_sems,
+    )
     columns = []
 
     def ready():
@@ -358,32 +376,33 @@
         scatter_rows(out_ref, value, in_ref.shape[0] // GROUP, first)
 
     group_products(in_ref, matrix_ref, ready, finish)
-
-
-def group_fwd_kernel(in_ref, matrices_hbm, out_ref, matrix_ref, sems):
-    copies = load([group_matrix(matrices_hbm, 1)], [matrix_ref], sems)
-
+    for copy in brought:
+        copy.wait()
+
+
+def group_fwd_kernel(in_ref, matrix_ref, out_ref):
     def finish(first, value):
         value = jnp.where(value < 0, value + MODULUS, value)
         value = jnp.where(value >= MODULUS, value - MODULUS, value)
         value = jnp.where(value < 0, value + MODULUS, value)
         scatter_rows(out_ref, value, in_ref.shape[0] // GROUP, first)
 
-    group_products(in_ref, matrix_ref, copies[0].wait, finish)
+    group_products(in_ref, matrix_ref, lambda: None, finish)
 
 
 def middle_kernel(
     in_ref,
+    side_back_ref,
+    mid_back_ref,
+    shift_ref,
     matrices_hbm,
     powers_hbm,
     made_hbm,
     out_ref,
-    side_back_ref,
-    mid_back_ref,
-    shift_ref,
+    group_fwd_ref,
+    side_back_t_ref,
     long_fwd_t_ref,
     mid_fwd_ref,
-    side_fwd_ref,
     ext_ref,
     sems,
 ):
@@ -391,25 +410,22 @@
     part = wide // SPLIT_OUT
     rows = SIDE // SPLIT_OUT
     cols = LONG // SPLIT_OUT
-    back = (((1,), (1,)), ((), ()))
     copies = load(
         [
-            matrices_hbm.at[pl.ds(wide, wide), pl.ds(0, wide)],
-            powers_hbm.at[pl.ds(2 * SIDE, SIDE)],
-            made_hbm.at[pl.ds(2 * SIDE, SIDE)],
+            matrices_hbm.at[pl.ds(3 * wide, wide)],
             matrices_hbm.at[pl.ds(0, wide)],
+            matrices_hbm.at[pl.ds(wide, wide)],
             powers_hbm.at[pl.ds(0, 2 * SIDE)],
-            matrices_hbm.at[pl.ds(wide, wide), pl.ds(wide, wide)],
             made_hbm.at[pl.ds(0, 2 * SIDE)],
+            group_matrix(matrices_hbm, 1),
         ],
         [
-            side_back_ref,
-            mid_back_ref,
-            shift_ref,
-            long_fwd_t_ref,
+            side_back_t_ref,
+            long_fwd_t_ref.at[pl.ds(0, wide)],
+            long_fwd_t_ref.at[pl.ds(wide, wide)],
             mid_fwd_ref,
-            side_fwd_ref,
             ext_ref,
+            group_fwd_ref,
         ],
         sems,
     )
@@ -425,33 +441,29 @@
         )
 
     def second(split):
-        return lax.dot_general(
-            split, side_back_ref[...], back, preferred_element_type=jnp.float32
-        )
+        return dot(split, side_back_t_ref[...])
 
     def after_second(k, result):
         here = slice(k * rows, (k + 1) * rows)
-        half = SIDE // SPLIT_OUT
-        result = jnp.concatenate(
-            [from_cols(result[:, n * part : (n + 1) * part], half) for n in range(SPLIT_OUT)], 1
-        )
+        result = from_cols(result, SIDE)
         return digits(paired_mul(result, shift_ref[here, 0:SIDE], shift_ref[here, SIDE:]), 1)
 
     split = digits(gather_rows(in_ref, SIDE, SIDE // LANES), 0)
-    for copy in copies[:3]:
-        copy.wait()
     one = first(0, split)
     two = first(1, split)
-    one = second(after_first(0, one))
-    two = second(after_first(1, two))
+    one = after_first(0, one)
+    copies[0].wait()
+    one = second(one)
+    two = after_first(1, two)
     one = after_second(0, one)
+    two = second(two)
     two = after_second(1, two)
     split = jnp.concatenate([one, two], 0)
-    for copy in copies[3:]:
-        copy.wait()
+    copies[1].wait()
+    copies[2].wait()
 
     def third(k):
-        return dot(split, long_fwd_t_ref[:, k * wide : (k + 1) * wide])
+        return dot(split, long_fwd_t_ref[k * wide : (k + 1) * wide, :])
 
     def after_third(k, result):
         here = slice(k * cols, (k + 1) * cols)
@@ -459,28 +471,48 @@
         return digits(paired_mul(result, mid_fwd_ref[0:SIDE, here], mid_fwd_ref[SIDE:, here]), 0)
 
     def fourth(split):
-        return dot(side_fwd_ref[...], split)
+        return dot(side_back_ref[...], split)
 
     def after_fourth(k, result):
         here = slice(k * cols, (k + 1) * cols)
-        result = from_rows(result, SIDE)
+        result = jnp.concatenate(
+            [from_rows(result[n * part : (n + 1) * part], rows) for n in range(SPLIT_OUT)], 0
+        )
         result = paired_mul(result, ext_ref[0:SIDE, here], ext_ref[SIDE:, here])
         scatter_rows(out_ref, result, LONG // LANES, k * cols // LANES)
 
     one = third(0)
+    for copy in copies[3:]:
+        copy.wait()
     two = third(1)
     one = fourth(after_third(0, one))
-    two = fourth(after_third(1, two))
+    two = after_third(1, two)
     after_fourth(0, one)
+    two = fourth(two)
     after_fourth(1, two)
 
 
-def limbs_kernel(in_ref, out_ref):
-    value = in_ref[...]
-    rows = in_ref.shape[0]
+def limbs_kernel(in_ref, out_hbm, out_ref, sems):
     scale = np.float32(1.0 / 65536.0)
-    out_ref[pl.ds(0, rows, stride=2), :] = (value & 65535).astype(jnp.float32) * scale
-    out_ref[pl.ds(1, rows, stride=2), :] = (value >> 16).astype(jnp.float32) * scale
+    per_line = LONG // LANES
+    parts = sems.shape[0]
+    rows = out_ref.shape[0] // parts
+    stores = []
+    for line in range(SIDE):
+        value = in_ref[pl.ds(-line % SIDE * per_line, per_line), :]
+        first = 2 * per_line * line
+        low = (value & 65535).astype(jnp.float32) * scale
+        high = (value >> 16).astype(jnp.float32) * scale
+        out_ref[pl.ds(first, per_line, stride=2), :] = low
+        out_ref[pl.ds(first + 1, per_line, stride=2), :] = high
+        done = first + 2 * per_line
+        if done % rows == 0:
+            part = pl.ds(done - rows, rows)
+            stores += load(
+                [out_ref.at[part]], [out_hbm.at[part]], sems.at[pl.ds(len(stores), 1)]
+            )
+    for copy in stores:
+        copy.wait()
 
 
 def exchange(rows):
@@ -504,17 +536,18 @@
     def limb(*shape):
         return jax.ShapeDtypeStruct(shape, jnp.bfloat16)
 
-    def call(name, body, out_shape, in_specs, scratch=(), sems=0, cost=1, out_spec=vmem):
+    def call(
+        name, body, out_shape, in_specs, scratch=(), sems=(), cost=1, out_specs=vmem, megabytes=48
+    ):
         scratch = [pltpu.VMEM(a.shape, a.dtype) for a in scratch]
-        if sems:
-            scratch.append(pltpu.SemaphoreType.DMA((sems,)))
+        scratch += [pltpu.SemaphoreType.DMA((count,)) for count in sems]
         return pl.pallas_call(
             body,
             out_shape=out_shape,
             in_specs=in_specs,
-            out_specs=out_spec,
+            out_specs=out_specs,
             scratch_shapes=scratch,
-            compiler_params=pltpu.CompilerParams(vmem_limit_bytes=48 << 20),
+            compiler_params=pltpu.CompilerParams(vmem_limit_bytes=megabytes << 20),
             cost_estimate=pl.CostEstimate(
                 flops=cost * 1_000_000, bytes_accessed=1 << 20, transcendentals=0
             ),
@@ -522,58 +555,61 @@
         )
 
     limbs = trace_limbs.reshape(2, rows, LANES).transpose(1, 0, 2).reshape(2 * rows, LANES)
-    values = call("join_limbs", join_kernel, ints(rows, LANES), [vmem])(limbs)
+    values = call(
+        "join_limbs",
+        join_kernel,
+        ints(rows, LANES),
+        [anywhere],
+        [limbs, ints(rows, LANES)],
+        (4, 4),
+        out_specs=anywhere,
+        megabytes=60,
+    )(limbs)
     made = call(
         "power_tables",
         table_kernel,
         ints(TABLE_ROWS, LONG),
         [smem, smem, anywhere],
         [ints(LINE_ROWS, LONG), ints(SIDE, LONG), ints(2 * SIDE, LONG)],
-        3,
+        (3,),
         300,
         anywhere,
     )(place, coset_shift, powers)
     columns = exchange(values)
-    columns = call(
+    columns, *brought = call(
         "group_back",
         group_back_kernel,
-        ints(rows, LANES),
+        [ints(rows, LANES), limb(wide, wide), ints(SIDE, LONG), ints(SIDE, LONG)],
         [smem, vmem, anywhere, anywhere, anywhere],
         [limb(LIMBS * GROUP, LIMBS * GROUP), ints(LINE_ROWS, LONG), ints(2 * GROUP, LONG)],
-        3,
+        (3, 3),
         300,
+        [vmem] * 4,
     )(place, columns, matrices, powers, made)
     block = exchange(columns)
-    extended = call(
+    extended, group_fwd = call(
         "block_transforms",
         middle_kernel,
-        ints(2 * rows, LANES),
-        [vmem, anywhere, anywhere, anywhere],
+        [ints(2 * rows, LANES), limb(LIMBS * GROUP, LIMBS * GROUP)],
+        [vmem] * 4 + [anywhere] * 3,
         [
             limb(wide, wide),
-            ints(SIDE, LONG),
-            ints(SIDE, LONG),
-            limb(wide, 2 * wide),
+            limb(2 * wide, wide),
             ints(2 * SIDE, LONG),
-            limb(wide, wide),
             ints(2 * SIDE, LONG),
         ],
-        7,
+        (6,),
         4000,
-    )(block, matrices, powers, made)
+        [vmem] * 2,
+    )(block, *brought, matrices, powers, made)
     columns = exchange(extended)
-    columns = call(
-        "group_fwd",
-        group_fwd_kernel,
-        ints(2 * rows, LANES),
-        [vmem, anywhere],
-        [limb(LIMBS * GROUP, LIMBS * GROUP)],
-        1,
-        500,
-    )(columns, matrices)
+    columns = call("group_fwd", group_fwd_kernel, ints(2 * rows, LANES), [vmem] * 2, cost=500)(
+        columns, group_fwd
+    )
     ordered = exchange(columns)
+    pairs = jax.ShapeDtypeStruct((4 * rows, LANES), jnp.float32)
     pairs = call(
-        "split_limbs", limbs_kernel, jax.ShapeDtypeStruct((4 * rows, LANES), jnp.float32), [vmem]
+        "split_limbs", limbs_kernel, pairs, [vmem], [pairs], (4,), out_specs=anywhere
     )(ordered)
     return pairs.reshape(2 * rows, 2, LANES).transpose(1, 0, 2).reshape(2, 2 * rows * LANES)
 

time: 128 us -> 126 us (0.984)
  no operation moved by 1% of the time
where the time goes in v2:
time: 126 us
  blocking collectives  75.5 us (60%)
  starting transfers between devices  19.4 us (15%)
  Pallas kernels  16.6 us (13%)
  waiting for transfers between devices  13.8 us (11%)
    all_to_all x3, blocking collectives, exchange(): lax.all_to_all(blocks, 'rows', split_axis=0, concat_axis=0, tiled=True)  75.5 us
    all_to_all x1, starting transfers between devices, exchange(): lax.all_to_all(blocks, 'rows', split_axis=0, concat_axis=0, tiled=True)  19.4 us
    all_to_all x1, waiting for transfers between devices, exchange(): lax.all_to_all(blocks, 'rows', split_axis=0, concat_axis=0, tiled=True)  13.8 us
    pallas_call x1, Pallas kernels, on_device(): call('block_transforms', middle_kernel, [ints(2 * rows, LANES), limb(LIMB...  6.53 us
    pallas_call x1, Pallas kernels, on_device(): call('power_tables', table_kernel, ints(TABLE_ROWS, LONG), [smem, smem, a...  3.19 us
    pallas_call x1, Pallas kernels, on_device(): call('group_back', group_back_kernel, [ints(rows, LANES), limb(wide, wide...  2.86 us
  transfers between devices with their start and end apart: 1, of which 1 were waited for; matrix products, arithmetic and copies ran while one was open for 0% of the time, Pallas kernels for 3%

profile of v2, /device:TPU:2, one launch (start us, length us, event | category | flops | bytes accessed | tf_op | source)
XLA Modules:
  0.0 126.2 jit_solution(3487335198473543376)
XLA Ops:
  0.0 1.8 %join_limbs.1 = s32[512,128]{1,0:T(8,128)} custom-call(f32[1024,128]{1,0:T(8,128)} %bitcast.27), custom_call_target="tpu_custom_call" | custom-call | flops 1000000 | bytes 1048576 | tf_op jit(solution)/shard_map/join_limbs/pallas_call | solution.py:558
  1.8 19.4 %all-to-all-start = ((s32[128,4,128]{2,1,0:T(4,128)}), s32[128,4,128]{2,1,0:T(4,128)S(1)}, u32[]{:S(2)}, u32[]{:S(2)}) async-start(s32[128,4,128]{2,1,0:T(4,128)} %bitcast.26), calls=%async_computation | async-start | bytes 524288 | tf_op jit(solution)/shard_map/all_to_all | solution.py:520
  21.9 3.2 %power_tables.1.made_hbm = s32[4096,512]{1,0:T(8,128)} custom-call(s32[1]{0:T(128)} %bitcast.place_ref, s32[1]{0:T(128)S(6)} %copy.7.shift_ref, s32[4096,512]{1,0:T(8,128)} %constant.11.clone.powers_hbm), custom_call_target="tpu_custom_call" | custom-call | flops 300000000 | bytes 1048576 | tf_op jit(solution)/shard_map/power_tables/pallas_call | solution.py:568
  25.1 13.8 %all-to-all-done = s32[128,4,128]{2,1,0:T(4,128)S(1)} async-done(((s32[128,4,128]{2,1,0:T(4,128)}), s32[128,4,128]{2,1,0:T(4,128)S(1)}, u32[]{:S(2)}, u32[]{:S(2)}) %all-to-all-start) | async-done | bytes 262176 | tf_op jit(solution)/shard_map/all_to_all | solution.py:520
  38.9 2.9 %group_back.1 = (s32[512,128]{1,0:T(8,128)S(1)}, bf16[1024,1024]{1,0:T(8,128)(2,1)S(1)}, s32[256,512]{1,0:T(8,128)S(1)}, s32[256,512]{1,0:T(8,128)S(1)}) custom-call(s32[1]{0:T(128)} %bitcast.place_ref, s32[512,128]{1,0:T(8,128)S(1)} %bitcast.20, bf16[4608,1024]{1,0:T(8,128)(2,1)} %constant.10.clone.matrices_hbm, s32[4096,512]{1,0:T(8,128)} %constant.11.clone.powers_hbm, ...), custom_call_target="tpu_custom_call" | custom-call | flops 300000000 | bytes 1048576 | tf_op jit(solution)/shard_map/group_back/pallas_call | solution.py:579
  41.7 21.9 %all_to_all.20 = s32[128,4,128]{2,1,0:T(4,128)S(1)} all-to-all(s32[128,4,128]{2,1,0:T(4,128)S(1)} %bitcast.25), channel_id=1, replica_groups=mesh['rows'=128,'cols'=4] {'rows'}, dimensions={0} | all-to-all | bytes 524288 | tf_op jit(solution)/shard_map/all_to_all | solution.py:520
  63.6 6.5 %block_transforms.1 = (s32[1024,128]{1,0:T(8,128)S(1)}, bf16[512,512]{1,0:T(8,128)(2,1)S(1)}) custom-call(s32[512,128]{1,0:T(8,128)S(1)} %bitcast.21, bf16[1024,1024]{1,0:T(8,128)(2,1)S(1)} %get-tuple-element.12.side_back_ref, s32[256,512]{1,0:T(8,128)S(1)} %get-tuple-element.13.mid_back_ref, s32[256,512]{1,0:T(8,128)S(1)} %get-tuple-element.14.shift_ref, ...), custom_call_target="tpu_custom_call" | custom-call | flops 4000000000 | bytes 1048576 | tf_op jit(solution)/shard_map/block_transforms/pallas_call | solution.py:590
  70.1 26.2 %all_to_all.21 = s32[128,8,128]{2,1,0:T(8,128)S(1)} all-to-all(s32[128,8,128]{2,1,0:T(8,128)S(1)} %bitcast.22), channel_id=1, replica_groups=mesh['rows'=128,'cols'=4] {'rows'}, dimensions={0} | all-to-all | bytes 1048576 | tf_op jit(solution)/shard_map/all_to_all | solution.py:520
  96.3 1.2 group_fwd.1
  97.5 27.4 %all_to_all.22 = s32[128,8,128]{2,1,0:T(8,128)S(1)} all-to-all(s32[128,8,128]{2,1,0:T(8,128)S(1)} %bitcast.24), channel_id=1, replica_groups=mesh['rows'=128,'cols'=4] {'rows'}, dimensions={0} | all-to-all | bytes 1048576 | tf_op jit(solution)/shard_map/all_to_all | solution.py:520
  124.9 1.1 split_limbs.1
Async XLA Ops:
  1.8 37.0 %all-to-all-start = ((s32[128,4,128]{2,1,0:T(4,128)}), s32[128,4,128]{2,1,0:T(4,128)S(1)}, u32[]{:S(2)}, u32[]{:S(2)}) async-start(s32[128,4,128]{2,1,0:T(4,128)} %bitcast.26), calls=%async_computation | async-start | bytes 524288 | tf_op jit(solution)/shard_map/all_to_all | solution.py:520

commit v3 on v2

--- a/solution.py
+++ b/solution.py
@@ -80,7 +80,7 @@
 
 
 SPLIT_OUT = 2
-MATRIX_ROWS = 4 * LIMBS * SIDE + LIMBS * GROUP
+MATRIX_ROWS = 3 * LIMBS * SIDE + LIMBS * GROUP
 TABLE_ROWS = 4096
 LINE_ROWS = 16
 LINES_AT = 1024
@@ -109,8 +109,7 @@
     matrices[:wide] = long_fwd[:wide].T
     matrices[wide : 2 * wide] = long_fwd[wide:].T
     matrices[2 * wide : 3 * wide] = in_parts(side_back, SIDE)
-    matrices[3 * wide : 4 * wide] = side_back.T
-    matrices[4 * wide :] = np.concatenate(
+    matrices[3 * wide :] = np.concatenate(
         [limb_matrix(dft_matrix(root, GROUP, GROUP)) for root in (back_group, root_group)], axis=1
     )
 
@@ -215,35 +214,38 @@
     return pl.ds(pl.multiple_of(LINES_AT + place * LINE_ROWS, LINE_ROWS), LINE_ROWS)
 
 
-def join_kernel(limbs_hbm, out_hbm, limbs_ref, out_ref, in_sems, out_sems):
-    parts = in_sems.shape[0]
-    rows = out_ref.shape[0] // parts
-    pairs = [pl.ds(2 * rows * k, 2 * rows) for k in range(parts)]
-    lines = [pl.ds(rows * k, rows) for k in range(parts)]
-    copies = load([limbs_hbm.at[r] for r in pairs], [limbs_ref.at[r] for r in pairs], in_sems)
-    stores = []
-    for k, copy in enumerate(copies):
-        copy.wait()
-        low = limbs_ref[pl.ds(2 * rows * k, rows, stride=2), :] * 65536.0
-        high = limbs_ref[pl.ds(2 * rows * k + 1, rows, stride=2), :] * 65536.0
-        joined = (high.astype(jnp.int32) << 16) + low.astype(jnp.int32)
-        out_ref[lines[k], :] = jnp.where(joined > HALF, joined - MODULUS, joined)
-        stores += load([out_ref.at[lines[k]]], [out_hbm.at[lines[k]]], out_sems.at[pl.ds(k, 1)])
-    for copy in stores:
-        copy.wait()
-
-
-def table_kernel(
-    place_ref, shift_ref, powers_hbm, out_hbm, own_ref, shift_table_ref, ext_ref, sems
+def tables_kernel(
+    place_ref,
+    shift_ref,
+    matrices_hbm,
+    powers_hbm,
+    group_back_ref,
+    base_ref,
+    own_ref,
+    side_back_ref,
+    mid_back_ref,
+    shift_cols_ref,
+    shift_rows_ref,
+    sems,
 ):
     place = place_ref[0]
-    own = load([powers_hbm.at[own_rows(place)]], [own_ref], sems.at[pl.ds(0, 1)])
+    copies = load(
+        [
+            group_matrix(matrices_hbm, 0),
+            powers_hbm.at[pl.ds(768, 2 * GROUP)],
+            powers_hbm.at[own_rows(place)],
+            matrices_hbm.at[pl.ds(2 * LIMBS * SIDE, LIMBS * SIDE)],
+            powers_hbm.at[pl.ds(2 * SIDE, SIDE)],
+        ],
+        [group_back_ref, base_ref, own_ref, side_back_ref, mid_back_ref],
+        sems,
+    )
 
     first = jnp.full((8, LANES), shift_ref[0], jnp.int32)
     square = jnp.where(first > HALF, first - MODULUS, first)
     inverse_len = int(centered(np.int64(pow(TRACE_LEN, MODULUS - 2, MODULUS))))
     factor = jnp.full((8, LANES), inverse_len, jnp.int32)
-    rows = lax.broadcasted_iota(jnp.int32, (SIDE, LANES), 0)
+    lines = lax.broadcasted_iota(jnp.int32, (SIDE, LANES), 0)
     column = jnp.ones((SIDE, LANES), jnp.int32)
     cols = lax.broadcasted_iota(jnp.int32, (8, SIDE), 1)
     line = None
@@ -254,7 +256,7 @@
         elif bit < 15:
             plain_row, lifted_row = square[0:1], lifted[0:1]
             column = jnp.where(
-                rows >> (bit - 7) & 1 == 1, near_mul(column, plain_row, lifted_row), column
+                lines >> (bit - 7) & 1 == 1, near_mul(column, plain_row, lifted_row), column
             )
         else:
             if line is None:
@@ -265,26 +267,21 @@
                 cols >> (bit - 15) & 1 == 1, near_mul(line, plain_row, lifted_row), line
             )
         square = near_mul(square, square, lifted)
-    line_lifted = lift(line)
-    for k in range(SIDE // LANES):
-        cols = slice(k * LANES, (k + 1) * LANES)
-        value = near_mul(column, line[0:1, cols], line_lifted[0:1, cols])
-        shift_table_ref[:, cols] = value
-        shift_table_ref[:, SIDE + k * LANES : SIDE + (k + 1) * LANES] = lift(value)
-    stores = load(
-        [shift_table_ref], [out_hbm.at[pl.ds(2 * SIDE, SIDE)]], sems.at[pl.ds(1, 1)]
-    )
-
-    own[0].wait()
-    column = as_column(own_ref[8:9, 0:SIDE])
-    for k in range(LONG // LANES):
-        cols = slice(k * LANES, (k + 1) * LANES)
-        value = near_mul(column, own_ref[0:1, cols], own_ref[1:2, cols])
-        ext_ref[0:SIDE, cols] = value
-        ext_ref[SIDE:, cols] = lift(value)
-    stores += load([ext_ref], [out_hbm.at[pl.ds(0, 2 * SIDE)]], sems.at[pl.ds(2, 1)])
-    for copy in stores:
+    shift_cols_ref[0:SIDE, :] = column
+    shift_cols_ref[SIDE:, :] = lift(column)
+    shift_rows_ref[0:8, :] = line
+    shift_rows_ref[8:16, :] = lift(line)
+
+    for copy in copies:
         copy.wait()
+
+
+def join_kernel(limbs_ref, after_ref, out_ref):
+    rows = out_ref.shape[0]
+    low = (limbs_ref[pl.ds(0, rows, stride=2), :] * 65536.0).astype(jnp.int32)
+    high = (limbs_ref[pl.ds(1, rows, stride=2), :] * 65536.0).astype(jnp.int32)
+    joined = (high << 16) + low
+    out_ref[...] = jnp.where(joined > HALF, joined - MODULUS, joined)
 
 
 def gather_rows(ref, lines, per_line):
@@ -301,10 +298,10 @@
 
 def group_matrix(matrices_hbm, index):
     size = LIMBS * GROUP
-    return matrices_hbm.at[pl.ds(4 * LIMBS * SIDE, size), pl.ds(index * size, size)]
-
-
-def group_products(in_ref, matrix_ref, ready, finish):
+    return matrices_hbm.at[pl.ds(3 * LIMBS * SIDE, size), pl.ds(index * size, size)]
+
+
+def group_products(in_ref, matrix_ref, finish):
     per_line = in_ref.shape[0] // GROUP
     step = 2
     splits = [
@@ -316,7 +313,6 @@
         )
         for first in range(0, per_line, step)
     ]
-    ready()
     last = None
     for index, split in enumerate(splits):
         result = dot(matrix_ref[...], split)
@@ -326,48 +322,11 @@
     finish((len(splits) - 1) * step, from_rows(last, GROUP))
 
 
-def group_back_kernel(
-    place_ref,
-    in_ref,
-    matrices_hbm,
-    powers_hbm,
-    made_hbm,
-    out_ref,
-    side_back_ref,
-    mid_back_ref,
-    shift_ref,
-    matrix_ref,
-    own_ref,
-    base_ref,
-    sems,
-    next_sems,
-):
-    copies = load(
-        [
-            group_matrix(matrices_hbm, 0),
-            powers_hbm.at[own_rows(place_ref[0])],
-            powers_hbm.at[pl.ds(768, 2 * GROUP)],
-        ],
-        [matrix_ref, own_ref, base_ref],
-        sems,
-    )
-    brought = load(
-        [
-            matrices_hbm.at[pl.ds(2 * LIMBS * SIDE, LIMBS * SIDE)],
-            powers_hbm.at[pl.ds(2 * SIDE, SIDE)],
-            made_hbm.at[pl.ds(2 * SIDE, SIDE)],
-        ],
-        [side_back_ref, mid_back_ref, shift_ref],
-        next_sems,
-    )
-    columns = []
-
-    def ready():
-        for copy in copies:
-            copy.wait()
-        for row in (8, 9):
-            column = as_column(own_ref[row : row + 1, SIDE : SIDE + LANES])
-            columns.append(jnp.concatenate([column, column], 1))
+def group_back_kernel(in_ref, matrix_ref, base_ref, own_ref, out_ref):
+    columns = [
+        jnp.concatenate([as_column(own_ref[row : row + 1, SIDE : SIDE + LANES])] * 2, 1)
+        for row in (8, 9)
+    ]
 
     def finish(first, value):
         cols = slice(first * LANES, first * LANES + value.shape[1])
@@ -375,9 +334,7 @@
         value = paired_mul(value, *columns)
         scatter_rows(out_ref, value, in_ref.shape[0] // GROUP, first)
 
-    group_products(in_ref, matrix_ref, ready, finish)
-    for copy in brought:
-        copy.wait()
+    group_products(in_ref, matrix_ref, finish)
 
 
 def group_fwd_kernel(in_ref, matrix_ref, out_ref):
@@ -387,23 +344,22 @@
         value = jnp.where(value < 0, value + MODULUS, value)
         scatter_rows(out_ref, value, in_ref.shape[0] // GROUP, first)
 
-    group_products(in_ref, matrix_ref, lambda: None, finish)
+    group_products(in_ref, matrix_ref, finish)
 
 
 def middle_kernel(
     in_ref,
     side_back_ref,
     mid_back_ref,
-    shift_ref,
+    shift_cols_ref,
+    shift_rows_ref,
+    own_ref,
     matrices_hbm,
     powers_hbm,
-    made_hbm,
     out_ref,
     group_fwd_ref,
-    side_back_t_ref,
     long_fwd_t_ref,
     mid_fwd_ref,
-    ext_ref,
     sems,
 ):
     wide = LIMBS * SIDE
@@ -412,19 +368,13 @@
     cols = LONG // SPLIT_OUT
     copies = load(
         [
-            matrices_hbm.at[pl.ds(3 * wide, wide)],
-            matrices_hbm.at[pl.ds(0, wide)],
-            matrices_hbm.at[pl.ds(wide, wide)],
+            matrices_hbm.at[pl.ds(0, 2 * wide)],
             powers_hbm.at[pl.ds(0, 2 * SIDE)],
-            made_hbm.at[pl.ds(0, 2 * SIDE)],
             group_matrix(matrices_hbm, 1),
         ],
         [
-            side_back_t_ref,
-            long_fwd_t_ref.at[pl.ds(0, wide)],
-            long_fwd_t_ref.at[pl.ds(wide, wide)],
+            long_fwd_t_ref,
             mid_fwd_ref,
-            ext_ref,
             group_fwd_ref,
         ],
         sems,
@@ -441,26 +391,50 @@
         )
 
     def second(split):
-        return dot(split, side_back_t_ref[...])
+        return [
+            dot(
+                split,
+                jnp.concatenate(
+                    [
+                        side_back_ref[
+                            n * part + b * rows : n * part + (b + 1) * rows,
+                            a * SIDE : (a + 1) * SIDE,
+                        ]
+                        for a in range(LIMBS)
+                        for n in range(SPLIT_OUT)
+                    ],
+                    0,
+                ),
+            )
+            for b in range(LIMBS)
+        ]
 
     def after_second(k, result):
         here = slice(k * rows, (k + 1) * rows)
-        result = from_cols(result, SIDE)
-        return digits(paired_mul(result, shift_ref[here, 0:SIDE], shift_ref[here, SIDE:]), 1)
-
+        result = combine(*result)
+        result = paired_mul(result, shift_rows_ref[0:1, :], shift_rows_ref[8:9, :])
+        lower = slice(SIDE + k * rows, SIDE + (k + 1) * rows)
+        columns = [
+            jnp.concatenate([shift_cols_ref[lines, :]] * (SIDE // LANES), 1)
+            for lines in (here, lower)
+        ]
+        return digits(paired_mul(result, *columns), 1)
+
+    ext_columns = [
+        jnp.concatenate([as_column(own_ref[row : row + 1, 0:SIDE])] * (cols // LANES), 1)
+        for row in (8, 9)
+    ]
     split = digits(gather_rows(in_ref, SIDE, SIDE // LANES), 0)
     one = first(0, split)
     two = first(1, split)
     one = after_first(0, one)
-    copies[0].wait()
     one = second(one)
     two = after_first(1, two)
     one = after_second(0, one)
     two = second(two)
     two = after_second(1, two)
     split = jnp.concatenate([one, two], 0)
-    copies[1].wait()
-    copies[2].wait()
+    copies[0].wait()
 
     def third(k):
         return dot(split, long_fwd_t_ref[k * wide : (k + 1) * wide, :])
@@ -478,11 +452,12 @@
         result = jnp.concatenate(
             [from_rows(result[n * part : (n + 1) * part], rows) for n in range(SPLIT_OUT)], 0
         )
-        result = paired_mul(result, ext_ref[0:SIDE, here], ext_ref[SIDE:, here])
+        result = paired_mul(result, own_ref[0:1, here], own_ref[1:2, here])
+        result = paired_mul(result, *ext_columns)
         scatter_rows(out_ref, result, LONG // LANES, k * cols // LANES)
 
     one = third(0)
-    for copy in copies[3:]:
+    for copy in copies[1:]:
         copy.wait()
     two = third(1)
     one = fourth(after_third(0, one))
@@ -555,53 +530,40 @@
         )
 
     limbs = trace_limbs.reshape(2, rows, LANES).transpose(1, 0, 2).reshape(2 * rows, LANES)
-    values = call(
-        "join_limbs",
-        join_kernel,
-        ints(rows, LANES),
-        [anywhere],
-        [limbs, ints(rows, LANES)],
-        (4, 4),
-        out_specs=anywhere,
-        megabytes=60,
-    )(limbs)
-    made = call(
+    group_back, base, own, side_back, mid_back, shift_cols, shift_rows = call(
         "power_tables",
-        table_kernel,
-        ints(TABLE_ROWS, LONG),
-        [smem, smem, anywhere],
-        [ints(LINE_ROWS, LONG), ints(SIDE, LONG), ints(2 * SIDE, LONG)],
-        (3,),
-        300,
-        anywhere,
-    )(place, coset_shift, powers)
+        tables_kernel,
+        [
+            limb(LIMBS * GROUP, LIMBS * GROUP),
+            ints(2 * GROUP, LONG),
+            ints(LINE_ROWS, LONG),
+            limb(wide, wide),
+            ints(SIDE, LONG),
+            ints(2 * SIDE, LANES),
+            ints(16, SIDE),
+        ],
+        [smem, smem] + [anywhere] * 2,
+        [],
+        (5,),
+        100,
+        [vmem] * 7,
+    )(place, coset_shift, matrices, powers)
+    values = call("join_limbs", join_kernel, ints(rows, LANES), [vmem] * 2)(limbs, shift_rows)
     columns = exchange(values)
-    columns, *brought = call(
-        "group_back",
-        group_back_kernel,
-        [ints(rows, LANES), limb(wide, wide), ints(SIDE, LONG), ints(SIDE, LONG)],
-        [smem, vmem, anywhere, anywhere, anywhere],
-        [limb(LIMBS * GROUP, LIMBS * GROUP), ints(LINE_ROWS, LONG), ints(2 * GROUP, LONG)],
-        (3, 3),
-        300,
-        [vmem] * 4,
-    )(place, columns, matrices, powers, made)
+    columns = call("group_back", group_back_kernel, ints(rows, LANES), [vmem] * 4, cost=300)(
+        columns, group_back, base, own
+    )
     block = exchange(columns)
     extended, group_fwd = call(
         "block_transforms",
         middle_kernel,
         [ints(2 * rows, LANES), limb(LIMBS * GROUP, LIMBS * GROUP)],
-        [vmem] * 4 + [anywhere] * 3,
-        [
-            limb(wide, wide),
-            limb(2 * wide, wide),
-            ints(2 * SIDE, LONG),
-            ints(2 * SIDE, LONG),
-        ],
-        (6,),
+        [vmem] * 6 + [anywhere] * 2,
+        [limb(2 * wide, wide), ints(2 * SIDE, LONG)],
+        (3,),
         4000,
         [vmem] * 2,
-    )(block, *brought, matrices, powers, made)
+    )(block, side_back, mid_back, shift_cols, shift_rows, own, matrices, powers)
     columns = exchange(extended)
     columns = call("group_fwd", group_fwd_kernel, ints(2 * rows, LANES), [vmem] * 2, cost=500)(
         columns, group_fwd

time: 126 us -> 125 us (level)
  blocking collectives: 75.5 us -> 112 us
  starting transfers between devices: 19.4 us -> 0 us
  waiting for transfers between devices: 13.8 us -> 0 us
  Pallas kernels: 16.6 us -> 11.3 us
    all_to_all x3 -> x4, blocking collectives: 75.5 us -> 112 us  [exchange(): lax.all_to_all(blocks, 'rows', split_axis=0, concat_axis=0, tiled=True)]
    all_to_all x1 -> x0, starting transfers between devices: 19.4 us -> none  [exchange(): lax.all_to_all(blocks, 'rows', split_axis=0, concat_axis=0, tiled=True)]
    all_to_all x1 -> x0, waiting for transfers between devices: 13.8 us -> none  [exchange(): lax.all_to_all(blocks, 'rows', split_axis=0, concat_axis=0, tiled=True)]
    pallas_call x3, Pallas kernels: 7.86 us -> 3.05 us  [the longest x1 2.11 us: on_device(): call('power_tables', tables_kernel, [limb(LIMBS * GROUP, LIMBS * GROUP),...]
  transfers between devices with their start and end apart: 1 -> 0, of which waited for: 1 -> 0; matrix products, arithmetic and copies ran while one was open for 0% -> 0% of each run, Pallas kernels for 3% -> 0%
where the time goes in v3:
time: 125 us
  blocking collectives  112 us (90%)
  Pallas kernels  11.3 us (9%)
    all_to_all x4, blocking collectives, exchange(): lax.all_to_all(blocks, 'rows', split_axis=0, concat_axis=0, tiled=True)  112 us
    pallas_call x1, Pallas kernels, on_device(): call('block_transforms', middle_kernel, [ints(2 * rows, LANES), limb(LIMB...  6.03 us

profile of v3, /device:TPU:2, one launch (start us, length us, event | category | flops | bytes accessed | tf_op | source)
XLA Modules:
  0.0 124.5 jit_solution(17549260312105561550)
XLA Ops:
  0.7 0.0 copy-start
  0.7 2.1 %power_tables.1 = (bf16[512,512]{1,0:T(8,128)(2,1)S(1)}, s32[256,512]{1,0:T(8,128)S(1)}, s32[16,512]{1,0:T(8,128)S(1)}, bf16[1024,1024]{1,0:T(8,128)(2,1)S(1)}, ...) custom-call(s32[1]{0:T(128)} %bitcast.3.place_ref, s32[1]{0:T(128)S(6)} %copy.7.shift_ref, ...), custom_call_target="tpu_custom_call" | custom-call | flops 100000000 | bytes 1048576 | tf_op jit(solution)/shard_map/power_tables/pallas_call | solution.py:533
  2.8 0.0 copy-done
  2.8 0.1 join_limbs.1
  2.9 36.8 %all_to_all.20 = s32[128,4,128]{2,1,0:T(4,128)S(1)} all-to-all(s32[128,4,128]{2,1,0:T(4,128)S(1)} %bitcast.23), channel_id=1, replica_groups=mesh['rows'=128,'cols'=4] {'rows'}, dimensions={0} | all-to-all | bytes 524288 | tf_op jit(solution)/shard_map/all_to_all | solution.py:495
  39.7 0.8 group_back.1
  40.6 21.9 %all_to_all.21 = s32[128,4,128]{2,1,0:T(4,128)S(1)} all-to-all(s32[128,4,128]{2,1,0:T(4,128)S(1)} %bitcast.22), channel_id=1, replica_groups=mesh['rows'=128,'cols'=4] {'rows'}, dimensions={0} | all-to-all | bytes 524288 | tf_op jit(solution)/shard_map/all_to_all | solution.py:495
  62.5 6.0 %block_transforms.1 = (s32[1024,128]{1,0:T(8,128)S(1)}, bf16[512,512]{1,0:T(8,128)(2,1)S(1)}) custom-call(s32[512,128]{1,0:T(8,128)S(1)} %bitcast.20, bf16[1024,1024]{1,0:T(8,128)(2,1)S(1)} %get-tuple-element.18.side_back_ref, s32[256,512]{1,0:T(8,128)S(1)} %get-tuple-element.19.mid_back_ref, s32[512,128]{1,0:T(8,128)S(1)} %get-tuple-element.20.shift_cols_ref, ...), custom_call_target="tpu_custom_call" | custom-call | flops 4000000000 | bytes 1048576 | tf_op jit(solution)/shard_map/block_transforms/pallas_call | solution.py:557
  68.5 26.2 %all_to_all.22 = s32[128,8,128]{2,1,0:T(8,128)S(1)} all-to-all(s32[128,8,128]{2,1,0:T(8,128)S(1)} %bitcast.25), channel_id=1, replica_groups=mesh['rows'=128,'cols'=4] {'rows'}, dimensions={0} | all-to-all | bytes 1048576 | tf_op jit(solution)/shard_map/all_to_all | solution.py:495
  94.7 1.2 group_fwd.1
  95.8 27.4 %all_to_all.23 = s32[128,8,128]{2,1,0:T(8,128)S(1)} all-to-all(s32[128,8,128]{2,1,0:T(8,128)S(1)} %bitcast.27), channel_id=1, replica_groups=mesh['rows'=128,'cols'=4] {'rows'}, dimensions={0} | all-to-all | bytes 1048576 | tf_op jit(solution)/shard_map/all_to_all | solution.py:495
  123.3 1.1 split_limbs.1
Async XLA Ops:
  0.7 2.2 %copy-start = (f32[2,65536]{1,0:T(2,128)S(1)}, f32[2,65536]{1,0:T(2,128)}, u32[]{:S(2)}) copy-start(f32[2,65536]{1,0:T(2,128)} %param.4) | copy-start | bytes 1572868

commit v4 on v3

--- a/solution.py
+++ b/solution.py
@@ -75,21 +75,11 @@
     )
 
 
-def dft_matrix(root, out_len, in_len):
-    return powers_of(root, np.arange(out_len)[:, None] * np.arange(in_len)[None, :])
-
-
-SPLIT_OUT = 2
-MATRIX_ROWS = 3 * LIMBS * SIDE + LIMBS * GROUP
+HALF_SIDE = SIDE // 2
+MATRIX_ROWS = 4096
 TABLE_ROWS = 4096
 LINE_ROWS = 16
 LINES_AT = 1024
-
-
-def in_parts(matrix, count):
-    rows, cols = matrix.shape
-    parts = matrix.reshape(LIMBS, SPLIT_OUT, count // SPLIT_OUT, cols).transpose(1, 0, 2, 3)
-    return parts.reshape(rows, cols)
 
 
 @functools.cache
@@ -98,20 +88,27 @@
     side = np.arange(SIDE)
     long = np.arange(LONG)
     tile = np.arange(LOCAL // GROUP)
+    half = np.arange(HALF_SIDE)
     back_side = pow(unity_root(SIDE), MODULUS - 2, MODULUS)
     root_group = unity_root(GROUP)
     back_group = pow(root_group, MODULUS - 2, MODULUS)
     back_local = pow(unity_root(LOCAL), MODULUS - 2, MODULUS)
-    side_back = limb_matrix(dft_matrix(back_side, SIDE, SIDE))
-    wide = LIMBS * SIDE
-    matrices = np.zeros((MATRIX_ROWS, wide), ml_dtypes.bfloat16)
-    long_fwd = in_parts(limb_matrix(dft_matrix(unity_root(LONG), LONG, SIDE)), LONG)
-    matrices[:wide] = long_fwd[:wide].T
-    matrices[wide : 2 * wide] = long_fwd[wide:].T
-    matrices[2 * wide : 3 * wide] = in_parts(side_back, SIDE)
-    matrices[3 * wide :] = np.concatenate(
-        [limb_matrix(dft_matrix(root, GROUP, GROUP)) for root in (back_group, root_group)], axis=1
-    )
+    small = LIMBS * HALF_SIDE
+
+    def product_matrix(root, outputs, inputs):
+        return limb_matrix(powers_of(root, outputs[:, None] * inputs[None, :]))
+
+    matrices = np.zeros((MATRIX_ROWS, 2 * small), ml_dtypes.bfloat16)
+    for parity in range(2):
+        long_fwd = product_matrix(unity_root(LONG), side, 2 * half + parity).T
+        long_fwd = long_fwd.reshape(small, LIMBS, 2, HALF_SIDE).transpose(0, 2, 1, 3)
+        matrices[parity * small : (parity + 1) * small] = long_fwd.reshape(small, 2 * small)
+        matrices[2 * small : 3 * small, parity * small : (parity + 1) * small] = product_matrix(
+            back_side, half, 2 * half + parity
+        )
+    matrices[3 * small : 4 * small, :small] = product_matrix(back_side, 2 * half + 1, half)
+    matrices[3 * small : 4 * small, small:] = product_matrix(root_group, lines, lines)
+    matrices[4 * small : 5 * small, :small] = product_matrix(back_group, lines, lines)
 
     powers = np.zeros((TABLE_ROWS, LONG), np.int32)
     powers[0:512] = both_halves(
@@ -130,7 +127,7 @@
         own[:, row : row + 2, lane : lane + exponents.size] = pair.transpose(1, 0, 2)
 
     place_pair(FWD_ROOT, long, 0, 0)
-    place_pair(FWD_ROOT, LONG * (-side % SIDE), 8, 0)
+    place_pair(FWD_ROOT, LONG * (-np.concatenate([2 * half, 2 * half + 1]) % SIDE), 8, 0)
     place_pair(BACK_ROOT, tile.size * lines, 8, SIDE)
     powers[LINES_AT : LINES_AT + GROUP * LINE_ROWS] = own.reshape(GROUP * LINE_ROWS, LONG)
     return matrices, powers
@@ -212,6 +209,11 @@
 
 def own_rows(place):
     return pl.ds(pl.multiple_of(LINES_AT + place * LINE_ROWS, LINE_ROWS), LINE_ROWS)
+
+
+def block_of(matrices_hbm, row, col):
+    size = LIMBS * HALF_SIDE
+    return matrices_hbm.at[pl.ds(row * size, size), pl.ds(col * size, size)]
 
 
 def tables_kernel(
@@ -229,12 +231,13 @@
     sems,
 ):
     place = place_ref[0]
+    small = LIMBS * HALF_SIDE
     copies = load(
         [
-            group_matrix(matrices_hbm, 0),
+            block_of(matrices_hbm, 4, 0),
             powers_hbm.at[pl.ds(768, 2 * GROUP)],
             powers_hbm.at[own_rows(place)],
-            matrices_hbm.at[pl.ds(2 * LIMBS * SIDE, LIMBS * SIDE)],
+            matrices_hbm.at[pl.ds(2 * small, small)],
             powers_hbm.at[pl.ds(2 * SIDE, SIDE)],
         ],
         [group_back_ref, base_ref, own_ref, side_back_ref, mid_back_ref],
@@ -248,6 +251,7 @@
     lines = lax.broadcasted_iota(jnp.int32, (SIDE, LANES), 0)
     column = jnp.ones((SIDE, LANES), jnp.int32)
     cols = lax.broadcasted_iota(jnp.int32, (8, SIDE), 1)
+    cols = (cols & (HALF_SIDE - 1)) * 2 + (cols >> 7)
     line = None
     for bit in range(23):
         lifted = lift(square)
@@ -296,11 +300,6 @@
         ref[pl.ds(first + k, lines, stride=per_line), :] = value[:, k * LANES : (k + 1) * LANES]
 
 
-def group_matrix(matrices_hbm, index):
-    size = LIMBS * GROUP
-    return matrices_hbm.at[pl.ds(3 * LIMBS * SIDE, size), pl.ds(index * size, size)]
-
-
 def group_products(in_ref, matrix_ref, finish):
     per_line = in_ref.shape[0] // GROUP
     step = 2
@@ -358,113 +357,154 @@
     powers_hbm,
     out_ref,
     group_fwd_ref,
-    long_fwd_t_ref,
+    long_fwd_ref,
+    side_odd_ref,
     mid_fwd_ref,
     sems,
 ):
-    wide = LIMBS * SIDE
-    part = wide // SPLIT_OUT
-    rows = SIDE // SPLIT_OUT
-    cols = LONG // SPLIT_OUT
+    small = LIMBS * HALF_SIDE
+    rows = HALF_SIDE
     copies = load(
         [
-            matrices_hbm.at[pl.ds(0, 2 * wide)],
+            matrices_hbm.at[pl.ds(0, 2 * small)],
             powers_hbm.at[pl.ds(0, 2 * SIDE)],
-            group_matrix(matrices_hbm, 1),
+            block_of(matrices_hbm, 3, 0),
+            block_of(matrices_hbm, 3, 1),
         ],
-        [
-            long_fwd_t_ref,
-            mid_fwd_ref,
-            group_fwd_ref,
-        ],
+        [long_fwd_ref, mid_fwd_ref, side_odd_ref, group_fwd_ref],
         sems,
     )
 
-    def first(k, split):
-        return dot(side_back_ref[k * part : (k + 1) * part, :], split)
-
-    def after_first(k, result):
-        here = slice(k * rows, (k + 1) * rows)
-        result = from_rows(result, rows)
-        return digits(
-            paired_mul(result, mid_back_ref[here, 0:SIDE], mid_back_ref[here, SIDE:]), 1
+    def wide_columns(ref, first):
+        return jnp.concatenate([ref[first : first + rows, :]] * (SIDE // LANES), 1)
+
+    per_line = SIDE // LANES
+    even, odd = (
+        dot(
+            side_back_ref[:, parity * small : (parity + 1) * small],
+            digits(
+                jnp.concatenate(
+                    [
+                        in_ref[pl.ds(per_line * parity + k, rows, stride=2 * per_line), :]
+                        for k in range(per_line)
+                    ],
+                    1,
+                ),
+                0,
+            ),
         )
-
-    def second(split):
-        return [
-            dot(
-                split,
+        for parity in range(2)
+    )
+
+    transposed = [
+        jnp.concatenate(
+            [
                 jnp.concatenate(
                     [
                         side_back_ref[
-                            n * part + b * rows : n * part + (b + 1) * rows,
-                            a * SIDE : (a + 1) * SIDE,
+                            b * rows : (b + 1) * rows,
+                            parity * small + a * rows : parity * small + (a + 1) * rows,
                         ]
                         for a in range(LIMBS)
-                        for n in range(SPLIT_OUT)
                     ],
                     0,
-                ),
+                )
+                for b in range(LIMBS)
+            ],
+            1,
+        )
+        for parity in range(2)
+    ]
+
+    def after_first(n, result):
+        here = slice(n * rows, (n + 1) * rows)
+        value = from_rows(result, rows)
+        value = near_mul(value, mid_back_ref[here, 0:SIDE], mid_back_ref[here, SIDE:])
+        left, right = value[:, 0:rows], value[:, rows:]
+        return [digits(left + right, 1), digits(left - right, 1)]
+
+    def second(splits):
+        return [dot(split, matrix) for split, matrix in zip(splits, transposed, strict=True)]
+
+    def after_second(n, results):
+        splits = []
+        for parity, result in enumerate(results):
+            here = slice(parity * rows, (parity + 1) * rows)
+            value = from_cols(result, rows)
+            value = paired_mul(value, shift_rows_ref[0:1, here], shift_rows_ref[8:9, here])
+            value = paired_mul(
+                value,
+                shift_cols_ref[n * rows : (n + 1) * rows, :],
+                shift_cols_ref[SIDE + n * rows : SIDE + (n + 1) * rows, :],
             )
-            for b in range(LIMBS)
-        ]
-
-    def after_second(k, result):
-        here = slice(k * rows, (k + 1) * rows)
-        result = combine(*result)
-        result = paired_mul(result, shift_rows_ref[0:1, :], shift_rows_ref[8:9, :])
-        lower = slice(SIDE + k * rows, SIDE + (k + 1) * rows)
-        columns = [
-            jnp.concatenate([shift_cols_ref[lines, :]] * (SIDE // LANES), 1)
-            for lines in (here, lower)
-        ]
-        return digits(paired_mul(result, *columns), 1)
-
-    ext_columns = [
-        jnp.concatenate([as_column(own_ref[row : row + 1, 0:SIDE])] * (cols // LANES), 1)
-        for row in (8, 9)
-    ]
-    split = digits(gather_rows(in_ref, SIDE, SIDE // LANES), 0)
-    one = first(0, split)
-    two = first(1, split)
-    one = after_first(0, one)
+            splits.append(digits(value, 1))
+        return splits
+
+    one = after_first(0, even + odd)
     one = second(one)
-    two = after_first(1, two)
+    two = after_first(1, even - odd)
     one = after_second(0, one)
     two = second(two)
     two = after_second(1, two)
-    split = jnp.concatenate([one, two], 0)
+    splits = [jnp.concatenate(pair, 0) for pair in zip(one, two, strict=True)]
     copies[0].wait()
 
     def third(k):
-        return dot(split, long_fwd_t_ref[k * wide : (k + 1) * wide, :])
-
-    def after_third(k, result):
-        here = slice(k * cols, (k + 1) * cols)
-        result = from_cols(result, cols)
-        return digits(paired_mul(result, mid_fwd_ref[0:SIDE, here], mid_fwd_ref[SIDE:, here]), 0)
-
-    def fourth(split):
-        return dot(side_back_ref[...], split)
-
-    def after_fourth(k, result):
-        here = slice(k * cols, (k + 1) * cols)
-        result = jnp.concatenate(
-            [from_rows(result[n * part : (n + 1) * part], rows) for n in range(SPLIT_OUT)], 0
+        return [
+            dot(
+                splits[parity],
+                long_fwd_ref[
+                    parity * small : (parity + 1) * small, k * small : (k + 1) * small
+                ],
+            )
+            for parity in range(2)
+        ]
+
+    def lanes_of(k):
+        return [slice(k * LANES, (k + 1) * LANES), slice(SIDE + k * LANES, SIDE + (k + 1) * LANES)]
+
+    def after_third(k, results):
+        even, odd = results
+        values = []
+        for here, result in zip(lanes_of(k), (even + odd, even - odd), strict=True):
+            value = from_cols(result, LANES)
+            values.append(near_mul(value, mid_fwd_ref[0:SIDE, here], mid_fwd_ref[SIDE:, here]))
+        value = jnp.concatenate(values, 1)
+        upper, lower = value[0:rows], value[rows:]
+        return [digits(upper + lower, 0), digits(upper - lower, 0)]
+
+    ext_columns = [as_column(own_ref[row : row + 1, 0:SIDE]) for row in (8, 9)]
+
+    def after_fourth(k, parity, result):
+        value = from_rows(result, rows)
+        plain, lifted = (
+            jnp.concatenate([own_ref[row : row + 1, here] for here in lanes_of(k)], 1)
+            for row in (0, 1)
         )
-        result = paired_mul(result, own_ref[0:1, here], own_ref[1:2, here])
-        result = paired_mul(result, *ext_columns)
-        scatter_rows(out_ref, result, LONG // LANES, k * cols // LANES)
+        value = paired_mul(value, plain, lifted)
+        value = paired_mul(
+            value, *(wide_columns(column, parity * rows) for column in ext_columns)
+        )
+        tiles = LONG // LANES
+        for n, tile in enumerate((k, SIDE // LANES + k)):
+            out_ref[pl.ds(parity * tiles + tile, rows, stride=2 * tiles), :] = value[
+                :, n * LANES : (n + 1) * LANES
+            ]
 
     one = third(0)
     for copy in copies[1:]:
         copy.wait()
     two = third(1)
-    one = fourth(after_third(0, one))
+    one = after_third(0, one)
+    by_parity = [side_back_ref[:, 0:small], side_odd_ref[...]]
+    one = [dot(matrix, split) for matrix, split in zip(by_parity, one, strict=True)]
     two = after_third(1, two)
-    after_fourth(0, one)
-    two = fourth(two)
-    after_fourth(1, two)
+    after_fourth(0, 0, one[0])
+    first = dot(by_parity[0], two[0])
+    after_fourth(0, 1, one[1])
+    last = dot(by_parity[1], two[1])
+    after_fourth(1, 0, first)
+    after_fourth(1, 1, last)
 
 
 def limbs_kernel(in_ref, out_hbm, out_ref, sems):
@@ -500,7 +540,7 @@
     matrices, powers = (jnp.asarray(table) for table in tables())
     place = lax.axis_index("rows").astype(jnp.int32).reshape(1)
     rows = LOCAL // LANES
-    wide = LIMBS * SIDE
+    small = LIMBS * HALF_SIDE
     smem = pl.BlockSpec(memory_space=pltpu.SMEM)
     vmem = pl.BlockSpec(memory_space=pltpu.VMEM)
     anywhere = pl.BlockSpec(memory_space=pl.ANY)
@@ -534,10 +574,10 @@
         "power_tables",
         tables_kernel,
         [
-            limb(LIMBS * GROUP, LIMBS * GROUP),
+            limb(small, small),
             ints(2 * GROUP, LONG),
             ints(LINE_ROWS, LONG),
-            limb(wide, wide),
+            limb(small, 2 * small),
             ints(SIDE, LONG),
             ints(2 * SIDE, LANES),
             ints(16, SIDE),
@@ -557,10 +597,10 @@
     extended, group_fwd = call(
         "block_transforms",
         middle_kernel,
-        [ints(2 * rows, LANES), limb(LIMBS * GROUP, LIMBS * GROUP)],
+        [ints(2 * rows, LANES), limb(small, small)],
         [vmem] * 6 + [anywhere] * 2,
-        [limb(2 * wide, wide), ints(2 * SIDE, LONG)],
-        (3,),
+        [limb(2 * small, 2 * small), limb(small, small), ints(2 * SIDE, LONG)],
+        (4,),
         4000,
         [vmem] * 2,
     )(block, side_back, mid_back, shift_cols, shift_rows, own, matrices, powers)

time: 125 us -> 124 us (level)
  no operation moved by 1% of the time
where the time goes in v4:
time: 124 us; the launch traced here: 123 us
  blocking collectives  112 us (90%)
  Pallas kernels  10.2 us (8%)
    all_to_all x4, blocking collectives, exchange(): lax.all_to_all(blocks, 'rows', split_axis=0, concat_axis=0, tiled=True)  112 us
    pallas_call x1, Pallas kernels, on_device(): call('block_transforms', middle_kernel, [ints(2 * rows, LANES), limb(smal...  5.18 us

profile of v4, /device:TPU:2, one launch (start us, length us, event | category | flops | bytes accessed | tf_op | source)
XLA Modules:
  0.0 123.3 jit_solution(9826359662398552517)
XLA Ops:
  0.7 0.0 copy-start
  0.7 1.8 %power_tables.1 = (bf16[512,512]{1,0:T(8,128)(2,1)S(1)}, s32[256,512]{1,0:T(8,128)S(1)}, s32[16,512]{1,0:T(8,128)S(1)}, bf16[512,1024]{1,0:T(8,128)(2,1)S(1)}, s...) custom-call(s32[1]{0:T(128)} %bitcast.3.place_ref, s32[1]{0:T(128)S(6)} %copy.7.shift_ref, ...), custom_call_target="tpu_custom_call" | custom-call | flops 100000000 | bytes 1048576 | tf_op jit(solution)/shard_map/power_tables/pallas_call | solution.py:573
  2.5 0.0 copy-done
  2.5 0.1 join_limbs.1
  2.6 36.8 %all_to_all.20 = s32[128,4,128]{2,1,0:T(4,128)S(1)} all-to-all(s32[128,4,128]{2,1,0:T(4,128)S(1)} %bitcast.23), channel_id=1, replica_groups=mesh['rows'=128,'cols'=4] {'rows'}, dimensions={0} | all-to-all | bytes 524288 | tf_op jit(solution)/shard_map/all_to_all | solution.py:535
  39.4 0.8 group_back.1
  40.3 21.9 %all_to_all.21 = s32[128,4,128]{2,1,0:T(4,128)S(1)} all-to-all(s32[128,4,128]{2,1,0:T(4,128)S(1)} %bitcast.22), channel_id=1, replica_groups=mesh['rows'=128,'cols'=4] {'rows'}, dimensions={0} | all-to-all | bytes 524288 | tf_op jit(solution)/shard_map/all_to_all | solution.py:535
  62.1 5.2 %block_transforms.1 = (s32[1024,128]{1,0:T(8,128)S(1)}, bf16[512,512]{1,0:T(8,128)(2,1)S(1)}) custom-call(s32[512,128]{1,0:T(8,128)S(1)} %bitcast.20, bf16[512,1024]{1,0:T(8,128)(2,1)S(1)} %get-tuple-element.18.side_back_ref, s32[256,512]{1,0:T(8,128)S(1)} %get-tuple-element.19.mid_back_ref, s32[512,128]{1,0:T(8,128)S(1)} %get-tuple-element.20.shift_cols_ref, ...), custom_call_target="tpu_custom_call" | custom-call | flops 4000000000 | bytes 1048576 | tf_op jit(solution)/shard_map/block_transforms/pallas_call | solution.py:597
  67.3 26.2 %all_to_all.22 = s32[128,8,128]{2,1,0:T(8,128)S(1)} all-to-all(s32[128,8,128]{2,1,0:T(8,128)S(1)} %bitcast.25), channel_id=1, replica_groups=mesh['rows'=128,'cols'=4] {'rows'}, dimensions={0} | all-to-all | bytes 1048576 | tf_op jit(solution)/shard_map/all_to_all | solution.py:535
  93.5 1.2 group_fwd.1
  94.7 27.4 %all_to_all.23 = s32[128,8,128]{2,1,0:T(8,128)S(1)} all-to-all(s32[128,8,128]{2,1,0:T(8,128)S(1)} %bitcast.27), channel_id=1, replica_groups=mesh['rows'=128,'cols'=4] {'rows'}, dimensions={0} | all-to-all | bytes 1048576 | tf_op jit(solution)/shard_map/all_to_all | solution.py:535
  122.1 1.1 split_limbs.1
Async XLA Ops:
  0.7 1.8 %copy-start = (f32[2,65536]{1,0:T(2,128)S(1)}, f32[2,65536]{1,0:T(2,128)}, u32[]{:S(2)}) copy-start(f32[2,65536]{1,0:T(2,128)} %param.4) | copy-start | bytes 1572868

commit v5 on v4

--- a/solution.py
+++ b/solution.py
@@ -107,8 +107,11 @@
             back_side, half, 2 * half + parity
         )
     matrices[3 * small : 4 * small, :small] = product_matrix(back_side, 2 * half + 1, half)
-    matrices[3 * small : 4 * small, small:] = product_matrix(root_group, lines, lines)
-    matrices[4 * small : 5 * small, :small] = product_matrix(back_group, lines, lines)
+    part = np.arange(GROUP // 2)
+    for row, col, root in ((3, 1, root_group), (4, 0, back_group)):
+        matrices[row * small : row * small + small // 2, col * small : (col + 1) * small] = (
+            np.concatenate([product_matrix(root, part, 2 * part + k) for k in range(2)], axis=1)
+        )
 
     powers = np.zeros((TABLE_ROWS, LONG), np.int32)
     powers[0:512] = both_halves(
@@ -211,14 +214,13 @@
     return pl.ds(pl.multiple_of(LINES_AT + place * LINE_ROWS, LINE_ROWS), LINE_ROWS)
 
 
-def block_of(matrices_hbm, row, col):
+def block_of(matrices_hbm, row, col, rows=LIMBS * HALF_SIDE):
     size = LIMBS * HALF_SIDE
-    return matrices_hbm.at[pl.ds(row * size, size), pl.ds(col * size, size)]
+    return matrices_hbm.at[pl.ds(row * size, rows), pl.ds(col * size, size)]
 
 
 def tables_kernel(
-    place_ref,
-    shift_ref,
+    shift_hbm,
     matrices_hbm,
     powers_hbm,
     group_back_ref,
@@ -228,23 +230,26 @@
     mid_back_ref,
     shift_cols_ref,
     shift_rows_ref,
+    shift_ref,
     sems,
 ):
-    place = place_ref[0]
+    place = lax.axis_index("rows")
     small = LIMBS * HALF_SIDE
     copies = load(
         [
-            block_of(matrices_hbm, 4, 0),
+            shift_hbm,
+            block_of(matrices_hbm, 4, 0, LIMBS * GROUP // 2),
             powers_hbm.at[pl.ds(768, 2 * GROUP)],
             powers_hbm.at[own_rows(place)],
             matrices_hbm.at[pl.ds(2 * small, small)],
             powers_hbm.at[pl.ds(2 * SIDE, SIDE)],
         ],
-        [group_back_ref, base_ref, own_ref, side_back_ref, mid_back_ref],
+        [shift_ref, group_back_ref, base_ref, own_ref, side_back_ref, mid_back_ref],
         sems,
     )
-
-    first = jnp.full((8, LANES), shift_ref[0], jnp.int32)
+    copies[0].wait()
+
+    first = jnp.broadcast_to(shift_ref[...], (8, LANES))
     square = jnp.where(first > HALF, first - MODULUS, first)
     inverse_len = int(centered(np.int64(pow(TRACE_LEN, MODULUS - 2, MODULUS))))
     factor = jnp.full((8, LANES), inverse_len, jnp.int32)
@@ -276,7 +281,7 @@
     shift_rows_ref[0:8, :] = line
     shift_rows_ref[8:16, :] = lift(line)
 
-    for copy in copies:
+    for copy in copies[1:]:
         copy.wait()
 
 
@@ -303,22 +308,30 @@
 def group_products(in_ref, matrix_ref, finish):
     per_line = in_ref.shape[0] // GROUP
     step = 2
-    splits = [
-        digits(
-            jnp.concatenate(
-                [in_ref[pl.ds(first + k, GROUP, stride=per_line), :] for k in range(step)], 1
-            ),
-            0,
-        )
-        for first in range(0, per_line, step)
-    ]
+    half = GROUP // 2
+    size = LIMBS * half
+
+    def split(first, parity):
+        lines = [
+            in_ref[pl.ds(per_line * parity + first + k, half, stride=2 * per_line), :]
+            for k in range(step)
+        ]
+        return digits(jnp.concatenate(lines, 1), 0)
+
+    def done(first, even, odd):
+        parts = [from_rows(result, half) for result in (even + odd, even - odd)]
+        finish(first, jnp.concatenate(parts, 0))
+
     last = None
-    for index, split in enumerate(splits):
-        result = dot(matrix_ref[...], split)
+    for first in range(0, per_line, step):
+        results = [
+            dot(matrix_ref[:, parity * size : (parity + 1) * size], split(first, parity))
+            for parity in range(2)
+        ]
         if last is not None:
-            finish((index - 1) * step, from_rows(last, GROUP))
-        last = result
-    finish((len(splits) - 1) * step, from_rows(last, GROUP))
+            done(first - step, *last)
+        last = results
+    done(per_line - step, *last)
 
 
 def group_back_kernel(in_ref, matrix_ref, base_ref, own_ref, out_ref):
@@ -369,7 +382,7 @@
             matrices_hbm.at[pl.ds(0, 2 * small)],
             powers_hbm.at[pl.ds(0, 2 * SIDE)],
             block_of(matrices_hbm, 3, 0),
-            block_of(matrices_hbm, 3, 1),
+            block_of(matrices_hbm, 3, 1, LIMBS * GROUP // 2),
         ],
         [long_fwd_ref, mid_fwd_ref, side_odd_ref, group_fwd_ref],
         sems,
@@ -538,7 +551,6 @@
 
 def on_device(trace_limbs, coset_shift):
     matrices, powers = (jnp.asarray(table) for table in tables())
-    place = lax.axis_index("rows").astype(jnp.int32).reshape(1)
     rows = LOCAL // LANES
     small = LIMBS * HALF_SIDE
     smem = pl.BlockSpec(memory_space=pltpu.SMEM)
@@ -574,7 +586,7 @@
         "power_tables",
         tables_kernel,
         [
-            limb(small, small),
+            limb(small // 2, small),
             ints(2 * GROUP, LONG),
             ints(LINE_ROWS, LONG),
             limb(small, 2 * small),
@@ -582,12 +594,12 @@
             ints(2 * SIDE, LANES),
             ints(16, SIDE),
         ],
-        [smem, smem] + [anywhere] * 2,
-        [],
-        (5,),
+        [anywhere] * 3,
+        [ints(1, 1)],
+        (6,),
         100,
         [vmem] * 7,
-    )(place, coset_shift, matrices, powers)
+    )(coset_shift.reshape(1, 1), matrices, powers)
     values = call("join_limbs", join_kernel, ints(rows, LANES), [vmem] * 2)(limbs, shift_rows)
     columns = exchange(values)
     columns = call("group_back", group_back_kernel, ints(rows, LANES), [vmem] * 4, cost=300)(
@@ -597,7 +609,7 @@
     extended, group_fwd = call(
         "block_transforms",
         middle_kernel,
-        [ints(2 * rows, LANES), limb(small, small)],
+        [ints(2 * rows, LANES), limb(small // 2, small)],
         [vmem] * 6 + [anywhere] * 2,
         [limb(2 * small, 2 * small), limb(small, small), ints(2 * SIDE, LONG)],
         (4,),

time: 124 us -> 123 us (level)
  no operation moved by 1% of the time
where the time goes in v5:
time: 123 us
  blocking collectives  112 us (91%)
  Pallas kernels  9.82 us (8%)
    all_to_all x4, blocking collectives, exchange(): lax.all_to_all(blocks, 'rows', split_axis=0, concat_axis=0, tiled=True)  112 us
    pallas_call x1, Pallas kernels, on_device(): call('block_transforms', middle_kernel, [ints(2 * rows, LANES), limb(smal...  5.09 us

profile of v5, /device:TPU:2, one launch (start us, length us, event | category | flops | bytes accessed | tf_op | source)
XLA Modules:
  0.0 123.0 jit_solution(9699482147916428673)
XLA Ops:
  0.7 0.0 copy-start
  0.7 1.7 %power_tables.1 = (bf16[256,512]{1,0:T(8,128)(2,1)S(1)}, s32[256,512]{1,0:T(8,128)S(1)}, s32[16,512]{1,0:T(8,128)S(1)}, bf16[512,1024]{1,0:T(8,128)(2,1)S(1)}, s...) custom-call(s32[1,1]{1,0:T(1,128)} %bitcast.19.shift_hbm, ...), custom_call_target="tpu_custom_call" | custom-call | flops 100000000 | bytes 1048576 | tf_op jit(solution)/shard_map/power_tables/pallas_call | solution.py:585
  2.4 0.0 copy-done
  2.4 0.1 join_limbs.1
  2.5 36.8 %all_to_all.20 = s32[128,4,128]{2,1,0:T(4,128)S(1)} all-to-all(s32[128,4,128]{2,1,0:T(4,128)S(1)} %bitcast.22), channel_id=1, replica_groups=mesh['rows'=128,'cols'=4] {'rows'}, dimensions={0} | all-to-all | bytes 524288 | tf_op jit(solution)/shard_map/all_to_all | solution.py:548
  39.3 0.7 group_back.1
  40.1 21.9 %all_to_all.21 = s32[128,4,128]{2,1,0:T(4,128)S(1)} all-to-all(s32[128,4,128]{2,1,0:T(4,128)S(1)} %bitcast.24), channel_id=1, replica_groups=mesh['rows'=128,'cols'=4] {'rows'}, dimensions={0} | all-to-all | bytes 524288 | tf_op jit(solution)/shard_map/all_to_all | solution.py:548
  62.0 5.1 %block_transforms.1 = (s32[1024,128]{1,0:T(8,128)S(1)}, bf16[256,512]{1,0:T(8,128)(2,1)S(1)}) custom-call(s32[512,128]{1,0:T(8,128)S(1)} %bitcast.21, bf16[512,1024]{1,0:T(8,128)(2,1)S(1)} %get-tuple-element.18.side_back_ref, s32[256,512]{1,0:T(8,128)S(1)} %get-tuple-element.19.mid_back_ref, s32[512,128]{1,0:T(8,128)S(1)} %get-tuple-element.20.shift_cols_ref, ...), custom_call_target="tpu_custom_call" | custom-call | flops 4000000000 | bytes 1048576 | tf_op jit(solution)/shard_map/block_transforms/pallas_call | solution.py:609
  67.1 26.2 %all_to_all.22 = s32[128,8,128]{2,1,0:T(8,128)S(1)} all-to-all(s32[128,8,128]{2,1,0:T(8,128)S(1)} %bitcast.26), channel_id=1, replica_groups=mesh['rows'=128,'cols'=4] {'rows'}, dimensions={0} | all-to-all | bytes 1048576 | tf_op jit(solution)/shard_map/all_to_all | solution.py:548
  93.2 1.1 group_fwd.1
  94.3 27.4 %all_to_all.23 = s32[128,8,128]{2,1,0:T(8,128)S(1)} all-to-all(s32[128,8,128]{2,1,0:T(8,128)S(1)} %bitcast.28), channel_id=1, replica_groups=mesh['rows'=128,'cols'=4] {'rows'}, dimensions={0} | all-to-all | bytes 1048576 | tf_op jit(solution)/shard_map/all_to_all | solution.py:548
  121.8 1.1 split_limbs.1
Async XLA Ops:
  0.7 1.8 %copy-start = (f32[2,65536]{1,0:T(2,128)S(1)}, f32[2,65536]{1,0:T(2,128)}, u32[]{:S(2)}) copy-start(f32[2,65536]{1,0:T(2,128)} %param.4) | copy-start | bytes 1572868

commit v6 on v5

--- a/solution.py
+++ b/solution.py
@@ -167,7 +167,7 @@
     return jnp.concatenate([part.astype(jnp.float32).astype(jnp.bfloat16) for part in parts], axis)
 
 
-def combine(part0, part1, part2, part3):
+def combine(part0, part1, part2, part3, whole_of=toward_zero):
     estimate = (
         part3 * np.float32(2.0**24 / MODULUS)
         + part2 * np.float32(2.0**16 / MODULUS)
@@ -175,15 +175,15 @@
     )
     whole = [part.astype(jnp.int32) for part in (part0, part1, part2, part3)]
     total = whole[0] + (whole[1] << 8) + (whole[2] << 16) + (whole[3] << 24)
-    return total - toward_zero(estimate) * MODULUS
+    return total - whole_of(estimate) * MODULUS
 
 
 def dot(left, right):
     return jnp.dot(left, right, preferred_element_type=jnp.float32)
 
 
-def from_rows(result, count):
-    return combine(*(result[k * count : (k + 1) * count] for k in range(LIMBS)))
+def from_rows(result, count, whole_of=toward_zero):
+    return combine(*(result[k * count : (k + 1) * count] for k in range(LIMBS)), whole_of=whole_of)
 
 
 def from_cols(result, count):
@@ -305,7 +305,7 @@
         ref[pl.ds(first + k, lines, stride=per_line), :] = value[:, k * LANES : (k + 1) * LANES]
 
 
-def group_products(in_ref, matrix_ref, finish):
+def group_products(in_ref, matrix_ref, finish, whole_of=toward_zero):
     per_line = in_ref.shape[0] // GROUP
     step = 2
     half = GROUP // 2
@@ -319,7 +319,7 @@
         return digits(jnp.concatenate(lines, 1), 0)
 
     def done(first, even, odd):
-        parts = [from_rows(result, half) for result in (even + odd, even - odd)]
+        parts = [from_rows(result, half, whole_of) for result in (even + odd, even - odd)]
         finish(first, jnp.concatenate(parts, 0))
 
     last = None
@@ -352,11 +352,9 @@
 def group_fwd_kernel(in_ref, matrix_ref, out_ref):
     def finish(first, value):
         value = jnp.where(value < 0, value + MODULUS, value)
-        value = jnp.where(value >= MODULUS, value - MODULUS, value)
-        value = jnp.where(value < 0, value + MODULUS, value)
         scatter_rows(out_ref, value, in_ref.shape[0] // GROUP, first)
 
-    group_products(in_ref, matrix_ref, finish)
+    group_products(in_ref, matrix_ref, finish, to_nearest)
 
 
 def middle_kernel(

time: 123 us -> 123 us (level)
  no operation moved by 1% of the time
where the time goes in v6:
time: 123 us
  blocking collectives  112 us (91%)
  Pallas kernels  9.75 us (8%)
    all_to_all x4, blocking collectives, exchange(): lax.all_to_all(blocks, 'rows', split_axis=0, concat_axis=0, tiled=True)  112 us
    pallas_call x1, Pallas kernels, on_device(): call('block_transforms', middle_kernel, [ints(2 * rows, LANES), limb(smal...  5.09 us

profile of v6, /device:TPU:2, one launch (start us, length us, event | category | flops | bytes accessed | tf_op | source)
XLA Modules:
  0.0 122.9 jit_solution(18129801384414654668)
XLA Ops:
  0.7 0.0 copy-start
  0.7 1.7 %power_tables.1 = (bf16[256,512]{1,0:T(8,128)(2,1)S(1)}, s32[256,512]{1,0:T(8,128)S(1)}, s32[16,512]{1,0:T(8,128)S(1)}, bf16[512,1024]{1,0:T(8,128)(2,1)S(1)}, s...) custom-call(s32[1,1]{1,0:T(1,128)} %bitcast.19.shift_hbm, ...), custom_call_target="tpu_custom_call" | custom-call | flops 100000000 | bytes 1048576 | tf_op jit(solution)/shard_map/power_tables/pallas_call | solution.py:583
  2.4 0.0 copy-done
  2.4 0.1 join_limbs.1
  2.5 36.8 %all_to_all.20 = s32[128,4,128]{2,1,0:T(4,128)S(1)} all-to-all(s32[128,4,128]{2,1,0:T(4,128)S(1)} %bitcast.22), channel_id=1, replica_groups=mesh['rows'=128,'cols'=4] {'rows'}, dimensions={0} | all-to-all | bytes 524288 | tf_op jit(solution)/shard_map/all_to_all | solution.py:546
  39.3 0.7 group_back.1
  40.1 21.9 %all_to_all.21 = s32[128,4,128]{2,1,0:T(4,128)S(1)} all-to-all(s32[128,4,128]{2,1,0:T(4,128)S(1)} %bitcast.24), channel_id=1, replica_groups=mesh['rows'=128,'cols'=4] {'rows'}, dimensions={0} | all-to-all | bytes 524288 | tf_op jit(solution)/shard_map/all_to_all | solution.py:546
  62.0 5.1 %block_transforms.1 = (s32[1024,128]{1,0:T(8,128)S(1)}, bf16[256,512]{1,0:T(8,128)(2,1)S(1)}) custom-call(s32[512,128]{1,0:T(8,128)S(1)} %bitcast.21, bf16[512,1024]{1,0:T(8,128)(2,1)S(1)} %get-tuple-element.18.side_back_ref, s32[256,512]{1,0:T(8,128)S(1)} %get-tuple-element.19.mid_back_ref, s32[512,128]{1,0:T(8,128)S(1)} %get-tuple-element.20.shift_cols_ref, ...), custom_call_target="tpu_custom_call" | custom-call | flops 4000000000 | bytes 1048576 | tf_op jit(solution)/shard_map/block_transforms/pallas_call | solution.py:607
  67.1 26.2 %all_to_all.22 = s32[128,8,128]{2,1,0:T(8,128)S(1)} all-to-all(s32[128,8,128]{2,1,0:T(8,128)S(1)} %bitcast.26), channel_id=1, replica_groups=mesh['rows'=128,'cols'=4] {'rows'}, dimensions={0} | all-to-all | bytes 1048576 | tf_op jit(solution)/shard_map/all_to_all | solution.py:546
  93.2 1.0 group_fwd.1
  94.3 27.4 %all_to_all.23 = s32[128,8,128]{2,1,0:T(8,128)S(1)} all-to-all(s32[128,8,128]{2,1,0:T(8,128)S(1)} %bitcast.28), channel_id=1, replica_groups=mesh['rows'=128,'cols'=4] {'rows'}, dimensions={0} | all-to-all | bytes 1048576 | tf_op jit(solution)/shard_map/all_to_all | solution.py:546
  121.7 1.1 split_limbs.1
Async XLA Ops:
  0.7 1.8 %copy-start = (f32[2,65536]{1,0:T(2,128)S(1)}, f32[2,65536]{1,0:T(2,128)}, u32[]{:S(2)}) copy-start(f32[2,65536]{1,0:T(2,128)} %param.4) | copy-start | bytes 1572868
